TPU v7x, 128 devices: a whole 4x4x4 slice. The times are simulated.
128 devices in a mesh: dp: 16 (over z, x), fsdp: 8 (over y, core).
Axes of the slice: x: 4, y: 4, z: 4, core: 2. Of those that a mesh axis runs over, the one named last changes fastest.
Arguments:
- feats: bfloat16 [256, 1024, 96], P(('dp', 'fsdp')), may hold values from -6 to 6
- targets: float32 [256, 1024], P(('dp', 'fsdp')), may hold values from -36 to 36
- lag_mask: int32 [256, 84], P(('dp', 'fsdp')), may hold values 0 or 1
- date_mask: int32 [256, 12], P(('dp', 'fsdp')), may hold values 0 or 1
- freq_ids: int32 [256], P(('dp', 'fsdp')), may hold values from 0 to 2
- dataset_ids: int32 [256], P(('dp', 'fsdp')), may hold values from 0 to 7
- w_in: bfloat16 [13824], P(('dp', 'fsdp')), may hold values from -0.625 to 0.625
- w_qkv: bfloat16 [62208], P(('dp', 'fsdp')), may hold values from -0.5 to 0.5
- w_out: bfloat16 [20736], P(('dp', 'fsdp')), may hold values from -2 to 2
- w_gu: bfloat16 [147456], P(('dp', 'fsdp')), may hold values from -0.5 to 0.5
- w_down: bfloat16 [73728], P(('dp', 'fsdp')), may hold values from -0.25 to 0.25
- gains: bfloat16 [2, 144], P(None, 'dp'), may hold values from 0.5 to 1.5
- running: float32 [8], replicated, may hold values from 0.5 to 4
- d_out: bfloat16 [256, 1024, 144], P(('dp', 'fsdp')), may hold values from -6 to 6
Outputs:
- out: bfloat16 [256, 1024, 144], P(('dp', 'fsdp'))
- grad_feats: bfloat16 [256, 1024, 96], P(('dp', 'fsdp'))
- grad_w_in: float32 [13824], P(('dp', 'fsdp'))
- grad_w_qkv: float32 [62208], P(('dp', 'fsdp'))
- grad_w_out: float32 [20736], P(('dp', 'fsdp'))
- grad_w_gu: float32 [147456], P(('dp', 'fsdp'))
- grad_w_down: float32 [73728], P(('dp', 'fsdp'))
- grad_gains: float32 [2, 144], P(None, 'dp')
- running_next: float32 [8], replicated
All inputs are finite; a program needn't handle non-finite values. Where the computation divides by a largest or mean magnitude, that divisor is 1e-20 or more. No bound on the sum of `lag_mask` or of `date_mask` on one device may be relied on, other than what follows from the above.
Results may differ from a plain program's by a relative error of at most 0.014.
Values may be sent and summed in bfloat16 or wider, within the bound.
A program may use at most 256 MiB of HBM per device.

v0:
```python
import jax
import jax.numpy as jnp
from jax import lax
from jax.sharding import PartitionSpec as P

D = 144
H = 9
HD = 16
FF = 512
NDATE = 12
F = 96
NSET = 8


norm_eps = 1e-05
scale_eps = 1e-05
momentum = 0.75
rope_base = 10000.0


def rope_angles(count, head_size):
    spots = jnp.arange(count, dtype=jnp.int32).astype(jnp.float32)
    freqs = rope_base ** (-jnp.arange(head_size // 2, dtype=jnp.float32) * 2.0 / head_size)
    angle = spots[:, None] * freqs[None, :]
    return (jnp.cos(angle), jnp.sin(angle))


def rotate(value, cos_part, sin_part):
    half = value.shape[-1] // 2
    front = value[..., :half]
    back = value[..., half:]
    cos_wide = cos_part[:, None, :]
    sin_wide = sin_part[:, None, :]
    return jnp.concatenate(
        [front * cos_wide - back * sin_wide, back * cos_wide + front * sin_wide], axis=-1
    )


def unrotate(grad, cos_part, sin_part):
    half = grad.shape[-1] // 2
    front = grad[..., :half]
    back = grad[..., half:]
    cos_wide = cos_part[:, None, :]
    sin_wide = sin_part[:, None, :]
    return jnp.concatenate(
        [front * cos_wide + back * sin_wide, back * cos_wide - front * sin_wide], axis=-1
    )


def unflatten(flats):
    return (
        flats[0].reshape(F, D),
        flats[1].reshape(D, 3 * D),
        flats[2].reshape(D, D),
        flats[3].reshape(D, 2 * FF),
        flats[4].reshape(FF, D),
    )


def norm_back(value, inverse, gain, grad):
    gain_grad = jnp.sum(grad * value * inverse, axis=(0, 1))
    inner = jnp.mean(grad * gain * value, axis=-1, keepdims=True)
    return (gain_grad, inverse * gain * grad - value * inverse * inverse * inverse * inner)


def project(left, right):
    return jnp.einsum("sti,ij->stj", left, right, preferred_element_type=jnp.float32)


def project_back(left, right):
    return jnp.einsum("stj,ij->sti", left, right, preferred_element_type=jnp.float32)


def outer_sum(left, right):
    return jnp.einsum("sti,stj->ij", left, right, preferred_element_type=jnp.float32)


def masked_scores(query, keys):
    length = query.shape[0]
    spots = jnp.arange(length, dtype=jnp.int32)
    allowed = spots[None, :] <= spots[:, None]
    raw = jnp.einsum("qhd,khd->hqk", query, keys, preferred_element_type=jnp.float32) * query.shape[
        -1
    ] ** (-0.5)
    return jnp.where(allowed[None], raw, -1e30)


def attend_series(item):
    query, keys, values = item
    scores = masked_scores(query, keys)
    total = jax.nn.logsumexp(scores, axis=-1, keepdims=True)
    weights = jnp.exp(scores - total).astype(jnp.bfloat16)
    mixed = jnp.einsum("hqk,khd->qhd", weights, values, preferred_element_type=jnp.float32)
    return (mixed.astype(jnp.bfloat16), total)


def attend_back(item):
    query, keys, values, grad_mixed, total = item
    scale_factor = query.shape[-1] ** (-0.5)
    scores = masked_scores(query, keys)
    chance = jnp.exp(scores - total)
    weights = chance.astype(jnp.bfloat16)
    grad_chance = jnp.einsum("qhd,khd->hqk", grad_mixed, values, preferred_element_type=jnp.float32)
    grad_scores = (
        chance * (grad_chance - jnp.sum(chance * grad_chance, axis=-1, keepdims=True))
    ).astype(jnp.bfloat16)
    grad_query = (
        jnp.einsum("hqk,khd->qhd", grad_scores, keys, preferred_element_type=jnp.float32)
        * scale_factor
    )
    grad_keys = (
        jnp.einsum("hqk,qhd->khd", grad_scores, query, preferred_element_type=jnp.float32)
        * scale_factor
    )
    grad_values = jnp.einsum(
        "hqk,qhd->khd", weights, grad_mixed, preferred_element_type=jnp.float32
    )
    return (grad_query, grad_keys, grad_values)


def body(
    feats,
    targets,
    lag_mask,
    date_mask,
    freq_ids,
    dataset_ids,
    w_in,
    w_qkv,
    w_out,
    w_gu,
    w_down,
    gains,
    running,
    d_out,
):
    count_seq, length, _ = feats.shape
    scale = jnp.mean(jnp.abs(targets), axis=1) + scale_eps
    shift_start = freq_ids * (NDATE // 3)
    keep = date_mask * (jnp.arange(NDATE, dtype=jnp.int32)[None, :] >= shift_start[:, None]).astype(
        jnp.int32
    )
    factors = jnp.concatenate(
        [lag_mask.astype(jnp.float32) / scale[:, None], keep.astype(jnp.float32)], axis=1
    )
    member = (dataset_ids[:, None] == jnp.arange(NSET, dtype=jnp.int32)[None, :]).astype(
        jnp.float32
    )
    set_sums = jnp.sum(member * scale[:, None], axis=0)
    set_counts = jnp.sum(member, axis=0)
    set_sums, set_counts = lax.psum((set_sums, set_counts), ("dp", "fsdp"))
    flats = (
        lax.all_gather(w_in, ("dp", "fsdp"), axis=0, tiled=True),
        lax.all_gather(w_qkv, ("dp", "fsdp"), axis=0, tiled=True),
        lax.all_gather(w_out, ("dp", "fsdp"), axis=0, tiled=True),
        lax.all_gather(w_gu, ("dp", "fsdp"), axis=0, tiled=True),
        lax.all_gather(w_down, ("dp", "fsdp"), axis=0, tiled=True),
    )
    matrix_in, matrix_qkv, matrix_out, matrix_gu, matrix_down = unflatten(flats)
    gain_full = lax.all_gather(gains, "dp", axis=1, tiled=True).astype(jnp.float32)
    lifted = (feats.astype(jnp.float32) * factors[:, None, :]).astype(jnp.bfloat16)
    first = project(lifted, matrix_in)
    inverse_one = lax.rsqrt(jnp.mean(first * first, axis=-1, keepdims=True) + norm_eps)
    normed = (first * inverse_one * gain_full[0]).astype(jnp.bfloat16)
    joint = project(normed, matrix_qkv)
    cos_part, sin_part = rope_angles(length, HD)
    query = rotate(joint[..., :D].reshape(count_seq, length, H, HD), cos_part, sin_part).astype(
        jnp.bfloat16
    )
    keys = rotate(
        joint[..., D : 2 * D].reshape(count_seq, length, H, HD), cos_part, sin_part
    ).astype(jnp.bfloat16)
    values = joint[..., 2 * D :].reshape(count_seq, length, H, HD).astype(jnp.bfloat16)
    mixed, totals = lax.map(attend_series, (query, keys, values))
    mixed = mixed.reshape(count_seq, length, D)
    middle = first + project(mixed, matrix_out)
    inverse_two = lax.rsqrt(jnp.mean(middle * middle, axis=-1, keepdims=True) + norm_eps)
    second = (middle * inverse_two * gain_full[1]).astype(jnp.bfloat16)
    both = project(second, matrix_gu)
    gate = both[..., :FF]
    up = both[..., FF:]
    hidden = (jax.nn.silu(gate) * up).astype(jnp.bfloat16)
    result = middle + project(hidden, matrix_down)
    out = result.astype(jnp.bfloat16)
    flats = (
        lax.all_gather(w_in, ("dp", "fsdp"), axis=0, tiled=True),
        lax.all_gather(w_qkv, ("dp", "fsdp"), axis=0, tiled=True),
        lax.all_gather(w_out, ("dp", "fsdp"), axis=0, tiled=True),
        lax.all_gather(w_gu, ("dp", "fsdp"), axis=0, tiled=True),
        lax.all_gather(w_down, ("dp", "fsdp"), axis=0, tiled=True),
    )
    matrix_in, matrix_qkv, matrix_out, matrix_gu, matrix_down = unflatten(flats)
    grad_down = outer_sum(hidden, d_out)
    grad_hidden = project_back(d_out, matrix_down)
    sigma = jax.nn.sigmoid(gate)
    grad_gate = grad_hidden * up * sigma * (1.0 + gate * (1.0 - sigma))
    grad_up = grad_hidden * gate * sigma
    grad_both = jnp.concatenate([grad_gate, grad_up], axis=-1).astype(jnp.bfloat16)
    grad_gu = outer_sum(second, grad_both)
    grad_second = project_back(grad_both, matrix_gu)
    gain_two, grad_norm_two = norm_back(middle, inverse_two, gain_full[1], grad_second)
    grad_middle = d_out.astype(jnp.float32) + grad_norm_two
    grad_branch = grad_middle.astype(jnp.bfloat16)
    grad_out = outer_sum(mixed, grad_branch)
    grad_mixed = (
        project_back(grad_branch, matrix_out).astype(jnp.bfloat16).reshape(count_seq, length, H, HD)
    )
    grad_query, grad_keys, grad_values = lax.map(
        attend_back, (query, keys, values, grad_mixed, totals)
    )
    grad_query = unrotate(grad_query, cos_part, sin_part).reshape(count_seq, length, D)
    grad_keys = unrotate(grad_keys, cos_part, sin_part).reshape(count_seq, length, D)
    grad_values = grad_values.reshape(count_seq, length, D)
    grad_joint = jnp.concatenate([grad_query, grad_keys, grad_values], axis=-1).astype(jnp.bfloat16)
    grad_qkv = outer_sum(normed, grad_joint)
    grad_normed = project_back(grad_joint, matrix_qkv)
    gain_one, grad_norm_one = norm_back(first, inverse_one, gain_full[0], grad_normed)
    grad_first = (grad_middle + grad_norm_one).astype(jnp.bfloat16)
    grad_in = outer_sum(lifted, grad_first)
    grad_lifted = project_back(grad_first, matrix_in)
    grad_feats = (grad_lifted * factors[:, None, :]).astype(jnp.bfloat16)
    owned = (
        lax.psum_scatter(grad_in.reshape(-1), ("dp", "fsdp"), scatter_dimension=0, tiled=True),
        lax.psum_scatter(grad_qkv.reshape(-1), ("dp", "fsdp"), scatter_dimension=0, tiled=True),
        lax.psum_scatter(grad_out.reshape(-1), ("dp", "fsdp"), scatter_dimension=0, tiled=True),
        lax.psum_scatter(grad_gu.reshape(-1), ("dp", "fsdp"), scatter_dimension=0, tiled=True),
        lax.psum_scatter(grad_down.reshape(-1), ("dp", "fsdp"), scatter_dimension=0, tiled=True),
    )
    gain_local = jnp.stack([gain_one, gain_two], axis=0)
    gain_total = lax.psum(gain_local, ("dp", "fsdp"))
    piece = D // lax.axis_size("dp")
    grad_gains = lax.dynamic_slice_in_dim(gain_total, lax.axis_index("dp") * piece, piece, 1)
    batch_mean = set_sums / jnp.maximum(set_counts, 1.0)
    running_next = jnp.where(
        set_counts > 0.5, momentum * running + (1.0 - momentum) * batch_mean, running
    )
    return (
        out,
        grad_feats,
        owned[0],
        owned[1],
        owned[2],
        owned[3],
        owned[4],
        grad_gains,
        running_next,
    )


def solution(mesh):
    in_specs = (
        P(("dp", "fsdp"), None, None),
        P(("dp", "fsdp"), None),
        P(("dp", "fsdp"), None),
        P(("dp", "fsdp"), None),
        P(("dp", "fsdp")),
        P(("dp", "fsdp")),
        P(("dp", "fsdp")),
        P(("dp", "fsdp")),
        P(("dp", "fsdp")),
        P(("dp", "fsdp")),
        P(("dp", "fsdp")),
        P(None, "dp"),
        P(),
        P(("dp", "fsdp"), None, None),
    )
    out_specs = (
        P(("dp", "fsdp"), None, None),
        P(("dp", "fsdp"), None, None),
        P(("dp", "fsdp")),
        P(("dp", "fsdp")),
        P(("dp", "fsdp")),
        P(("dp", "fsdp")),
        P(("dp", "fsdp")),
        P(None, "dp"),
        P(),
    )
    return jax.shard_map(body, mesh=mesh, in_specs=in_specs, out_specs=out_specs, check_vma=False)
```

profile of v0, /device:TPU:1, one launch (start us, length us, event | category | flops | bytes accessed | tf_op | source)
XLA Modules:
  0.0 882.7 jit_solution(5837434361901477468)
XLA Ops:
  16.6 18.3 %all-gather = bf16[16,9,2]{1,2,0:T(2,128)(2,1)S(1)} all-gather(bf16[1,9,2]{1,2,0:T(2,128)(2,1)} %bitcast.204), channel_id=1, replica_groups=mesh['dp'=16,'fsdp'=8] {'dp'}, dimensions={0}, use_global_device_ids=true | all-gather | bytes 612 | tf_op jit(solution)/shard_map/all_gather | solution.py:160
  35.7 40.4 %all-gather.1 = bf16[128,1,1152]{2,1,0:T(2,128)(2,1)S(1)} all-gather(bf16[1,1,1152]{2,1,0:T(2,128)(2,1)S(1)} %reshape.269), channel_id=1, replica_groups=mesh['dp'=16,'fsdp'=8] {'dp','fsdp'}, dimensions={0}, use_global_device_ids=true | all-gather | bytes 297216 | tf_op jit(solution)/shard_map/all_gather | solution.py:156
  79.3 75.6 %all-reduce.19.cloned.1.call-done = (bf16[13824]{0:T(1024)(128)(2,1)}, bf16[20736]{0:T(1024)(128)(2,1)}) async-done(((bf16[13824]{0:T(1024)(128)(2,1)}, bf16[20736]{0:T(1024)(128)(2,1)}), (bf16[13824]{0:T(1024)(128)(2,1)}, bf16[20736]{0:T(1024)(128)(2,1)})) %all-reduce.19.cloned.1.call-update) | async-done | bytes 69136
  159.3 140.4 %all-reduce.21.cloned.1.call-done = (bf16[62208]{0:T(1024)(128)(2,1)}, bf16[73728]{0:T(1024)(128)(2,1)}) async-done(((bf16[62208]{0:T(1024)(128)(2,1)}, bf16[73728]{0:T(1024)(128)(2,1)}), (bf16[62208]{0:T(1024)(128)(2,1)}, bf16[73728]{0:T(1024)(128)(2,1)})) %all-reduce.21.cloned.1.call-update) | async-done | bytes 271888
  306.0 97.1 %while.26 = (s32[]{:T(128)}, bf16[2,1024,9,16]{1,3,2,0:T(8,128)(2,1)S(1)}, f32[2,9,1024,1]{2,1,3,0:T(8,128)S(1)}, bf16[2,1024,9,16]{1,3,2,0:T(8,128)(2,1)}, bf16...) while((s32[]{:T(128)}, bf16[2,1024,9,16]{1,3,2,0:T(8,128)(2,1)S(1)}, ...), condition=%wide.region_5.0_spmd, body=%wide.region_2.5_spmd.sunk | while | flops 709058560 | bytes 119179344 | solution.py:174
  306.7 15.2 %fusion.119 = (f32[9,1024]{1,0:T(8,128)S(1)}, f32[9,1024,1024]{1,2,0:T(8,128)}) fusion(pred[1024,1024]{0,1:T(8,128)(4,1)S(1)} %iota_compare_fusion.5, bf16[2,1024,9,16]{1,3,2,0:T(8,128)(2,1)S(1)} %get-tuple-element.296, s32[]{:T(128)S(6)} %copy.152, bf16[2,1024,9,16]{1,3,2,0:T(8,128)(2,1)S(1)} %get-tuple-element.295), kind=kOutput, calls=%fused_computation.3.clone.1 | convolution fusion | flops 330292224 | bytes 39425024 | tf_op jit(solution)/shard_map/while/body/eval_jaxpr/qhd,khd->hqk/dot_general | solution.py:82
  321.9 16.6 %exponential_reduce_fusion.2 = f32[9,1024]{1,0:T(8,128)S(1)} fusion(f32[9,1024,1024]{1,2,0:T(8,128)} %get-tuple-element.264, f32[9,1024]{1,0:T(8,128)S(1)} %is-finite_select_fusion.3, pred[1024,1024]{0,1:T(8,128)(4,1)S(1)} %iota_compare_fusion.5), kind=kLoop, calls=%fused_computation.1.clone.1 | loop fusion | flops 37739520 | bytes 38871040 | tf_op jit(solution)/shard_map/while/body/eval_jaxpr/reduce_sum | solution.py:91
  338.5 16.2 %fusion.121 = bf16[2,1024,9,16]{1,3,2,0:T(8,128)(2,1)S(1)} fusion(bf16[2,1024,9,16]{1,3,2,0:T(8,128)(2,1)S(1)} %get-tuple-element.285, s32[]{:T(128)S(6)} %copy.152, f32[9,1024,1024]{1,2,0:T(8,128)} %get-tuple-element.264, f32[9,1024]{1,0:T(8,128)S(1)} %fusion.120, pred[1024,1024]{0,1:T(8,128)(4,1)S(1)} %iota_compare_fusion.5, ...), kind=kOutput, calls=%fused_computation.9.clone.1 | convolution fusion | flops 339886080 | bytes 39453696 | tf_op jit(solution)/shard_map/while/body/eval_jaxpr/hqk,khd->qhd/dot_general | solution.py:93
  355.1 15.2 %fusion.119 = (f32[9,1024]{1,0:T(8,128)S(1)}, f32[9,1024,1024]{1,2,0:T(8,128)}) fusion(pred[1024,1024]{0,1:T(8,128)(4,1)S(1)} %iota_compare_fusion.5, bf16[2,1024,9,16]{1,3,2,0:T(8,128)(2,1)S(1)} %get-tuple-element.296, s32[]{:T(128)S(6)} %copy.152, bf16[2,1024,9,16]{1,3,2,0:T(8,128)(2,1)S(1)} %get-tuple-element.295), kind=kOutput, calls=%fused_computation.3.clone.1 | convolution fusion | flops 330292224 | bytes 39425024 | tf_op jit(solution)/shard_map/while/body/eval_jaxpr/qhd,khd->hqk/dot_general | solution.py:82
  370.2 16.6 %exponential_reduce_fusion.2 = f32[9,1024]{1,0:T(8,128)S(1)} fusion(f32[9,1024,1024]{1,2,0:T(8,128)} %get-tuple-element.264, f32[9,1024]{1,0:T(8,128)S(1)} %is-finite_select_fusion.3, pred[1024,1024]{0,1:T(8,128)(4,1)S(1)} %iota_compare_fusion.5), kind=kLoop, calls=%fused_computation.1.clone.1 | loop fusion | flops 37739520 | bytes 38871040 | tf_op jit(solution)/shard_map/while/body/eval_jaxpr/reduce_sum | solution.py:91
  386.9 16.2 %fusion.121 = bf16[2,1024,9,16]{1,3,2,0:T(8,128)(2,1)S(1)} fusion(bf16[2,1024,9,16]{1,3,2,0:T(8,128)(2,1)S(1)} %get-tuple-element.285, s32[]{:T(128)S(6)} %copy.152, f32[9,1024,1024]{1,2,0:T(8,128)} %get-tuple-element.264, f32[9,1024]{1,0:T(8,128)S(1)} %fusion.120, pred[1024,1024]{0,1:T(8,128)(4,1)S(1)} %iota_compare_fusion.5, ...), kind=kOutput, calls=%fused_computation.9.clone.1 | convolution fusion | flops 339886080 | bytes 39453696 | tf_op jit(solution)/shard_map/while/body/eval_jaxpr/hqk,khd->qhd/dot_general | solution.py:93
  405.5 3.6 fusion.59
  409.1 2.4 fusion.65
  415.0 231.0 %while.27 = (s32[]{:T(128)}, f32[2,1024,9,16]{1,3,2,0:T(8,128)}, f32[2,1024,9,16]{1,3,2,0:T(8,128)}, bf16[2,1024,9,16]{1,3,2,0:T(8,128)(2,1)}, bf16[2,1024,9,16]...) while((s32[]{:T(128)}, f32[2,1024,9,16]{1,3,2,0:T(8,128)}, ...), condition=%wide.region_10.11_spmd, body=%wide.region_8.0_spmd.sunk | while | flops 1652841472 | bytes 294413504 | solution.py:208
  426.4 14.7 %fusion.131 = f32[9,1024,1024]{1,2,0:T(8,128)} fusion(bf16[2,1024,9,16]{1,3,2,0:T(8,128)(2,1)S(1)} %get-tuple-element.323, s32[]{:T(128)S(6)} %copy.162, bf16[2,1024,9,16]{1,3,2,0:T(8,128)(2,1)S(1)} %get-tuple-element.322), kind=kOutput, calls=%fused_computation.47.clone.1 | convolution fusion | flops 301989888 | bytes 38339584 | tf_op jit(solution)/shard_map/while/body/eval_jaxpr/qhd,khd->hqk/dot_general | solution.py:82
  441.2 15.5 %fusion.134 = bf16[2,1024,9,16]{1,3,2,0:T(8,128)(2,1)} fusion(bf16[2,1024,9,16]{1,3,2,0:T(8,128)(2,1)} %get-tuple-element.311, s32[]{:T(128)S(6)} %copy.162, f32[9,1024,1024]{1,2,0:T(8,128)} %fusion.131, f32[9,1024]{1,0:T(8,128)S(1)} %dynamic-slice_bitcast_fusion.2, pred[1024,1024]{0,1:T(8,128)(4,1)S(1)} %iota_compare_fusion.6, ...), kind=kOutput, calls=%fused_computation.41.clone.1 | convolution fusion | flops 339738624 | bytes 39748608 | tf_op jit(solution)/shard_map/while/body/eval_jaxpr/hqk,qhd->khd/dot_general | solution.py:115
  456.7 25.8 %multiply_reduce_fusion.8 = (f32[9,1024]{1,0:T(8,128)S(1)}, f32[9,1024,1024]{1,2,0:T(8,128)}) fusion(f32[9,1024,1024]{1,2,0:T(8,128)} %fusion.131, f32[9,1024]{1,0:T(8,128)S(1)} %dynamic-slice_bitcast_fusion.2, pred[1024,1024]{0,1:T(8,128)(4,1)S(1)} %iota_compare_fusion.6, bf16[2,1024,9,16]{1,3,2,0:T(8,128)(2,1)S(1)} %copy-done.7, s32[]{:T(128)S(6)} %copy.162, ...), kind=kOutput, calls=%fused_computation.28.clone.1 | convolution fusion | flops 349166592 | bytes 77239296 | tf_op jit(solution)/shard_map/while/body/eval_jaxpr/qhd,khd->hqk/dot_general | solution.py:103
  482.5 31.4 %multiply_convert_fusion.12 = bf16[9,1024,1024]{1,2,0:T(8,128)(2,1)} fusion(f32[9,1024,1024]{1,2,0:T(8,128)} %get-tuple-element.275, f32[9,1024,1024]{1,2,0:T(8,128)} %fusion.131, f32[9,1024]{1,0:T(8,128)S(1)} %get-tuple-element.276, f32[9,1024]{1,0:T(8,128)S(1)} %dynamic-slice_bitcast_fusion.2, pred[1024,1024]{0,1:T(8,128)(4,1)S(1)} %iota_compare_fusion.6), kind=kLoop, calls=%fused_computation.27.clone.1 | loop fusion | flops 56623104 | bytes 95494144 | tf_op jit(solution)/shard_map/while/body/eval_jaxpr/convert_element_type | solution.py:106
  513.9 12.2 %fusion.133 = f32[2,1024,9,16]{1,3,2,0:T(8,128)} fusion(f32[2,1024,9,16]{1,3,2,0:T(8,128)} %get-tuple-element.310, s32[]{:T(128)S(6)} %copy.162, bf16[9,1024,1024]{1,2,0:T(8,128)(2,1)} %multiply_convert_fusion.12, bf16[2,1024,9,16]{1,3,2,0:T(8,128)(2,1)S(1)} %get-tuple-element.323), kind=kOutput, calls=%fused_computation.39.clone.1 | convolution fusion | flops 302137344 | bytes 19760128 | tf_op jit(solution)/shard_map/while/body/eval_jaxpr/hqk,qhd->khd/dot_general | solution.py:112
  526.1 9.8 %fusion.132 = f32[2,1024,9,16]{1,3,2,0:T(8,128)} fusion(f32[2,1024,9,16]{1,3,2,0:T(8,128)} %get-tuple-element.309, s32[]{:T(128)S(6)} %copy.162, bf16[9,1024,1024]{1,2,0:T(8,128)(2,1)} %multiply_convert_fusion.12, bf16[2,1024,9,16]{1,3,2,0:T(8,128)(2,1)S(1)} %get-tuple-element.322), kind=kOutput, calls=%fused_computation.37.clone.1 | convolution fusion | flops 302137344 | bytes 19760128 | tf_op jit(solution)/shard_map/while/body/eval_jaxpr/hqk,khd->qhd/dot_general | solution.py:108
  536.5 14.7 %fusion.131 = f32[9,1024,1024]{1,2,0:T(8,128)} fusion(bf16[2,1024,9,16]{1,3,2,0:T(8,128)(2,1)S(1)} %get-tuple-element.323, s32[]{:T(128)S(6)} %copy.162, bf16[2,1024,9,16]{1,3,2,0:T(8,128)(2,1)S(1)} %get-tuple-element.322), kind=kOutput, calls=%fused_computation.47.clone.1 | convolution fusion | flops 301989888 | bytes 38339584 | tf_op jit(solution)/shard_map/while/body/eval_jaxpr/qhd,khd->hqk/dot_general | solution.py:82
  551.3 15.5 %fusion.134 = bf16[2,1024,9,16]{1,3,2,0:T(8,128)(2,1)} fusion(bf16[2,1024,9,16]{1,3,2,0:T(8,128)(2,1)} %get-tuple-element.311, s32[]{:T(128)S(6)} %copy.162, f32[9,1024,1024]{1,2,0:T(8,128)} %fusion.131, f32[9,1024]{1,0:T(8,128)S(1)} %dynamic-slice_bitcast_fusion.2, pred[1024,1024]{0,1:T(8,128)(4,1)S(1)} %iota_compare_fusion.6, ...), kind=kOutput, calls=%fused_computation.41.clone.1 | convolution fusion | flops 339738624 | bytes 39748608 | tf_op jit(solution)/shard_map/while/body/eval_jaxpr/hqk,qhd->khd/dot_general | solution.py:115
  566.8 25.8 %multiply_reduce_fusion.8 = (f32[9,1024]{1,0:T(8,128)S(1)}, f32[9,1024,1024]{1,2,0:T(8,128)}) fusion(f32[9,1024,1024]{1,2,0:T(8,128)} %fusion.131, f32[9,1024]{1,0:T(8,128)S(1)} %dynamic-slice_bitcast_fusion.2, pred[1024,1024]{0,1:T(8,128)(4,1)S(1)} %iota_compare_fusion.6, bf16[2,1024,9,16]{1,3,2,0:T(8,128)(2,1)S(1)} %copy-done.7, s32[]{:T(128)S(6)} %copy.162, ...), kind=kOutput, calls=%fused_computation.28.clone.1 | convolution fusion | flops 349166592 | bytes 77239296 | tf_op jit(solution)/shard_map/while/body/eval_jaxpr/qhd,khd->hqk/dot_general | solution.py:103
  592.6 31.4 %multiply_convert_fusion.12 = bf16[9,1024,1024]{1,2,0:T(8,128)(2,1)} fusion(f32[9,1024,1024]{1,2,0:T(8,128)} %get-tuple-element.275, f32[9,1024,1024]{1,2,0:T(8,128)} %fusion.131, f32[9,1024]{1,0:T(8,128)S(1)} %get-tuple-element.276, f32[9,1024]{1,0:T(8,128)S(1)} %dynamic-slice_bitcast_fusion.2, pred[1024,1024]{0,1:T(8,128)(4,1)S(1)} %iota_compare_fusion.6), kind=kLoop, calls=%fused_computation.27.clone.1 | loop fusion | flops 56623104 | bytes 95494144 | tf_op jit(solution)/shard_map/while/body/eval_jaxpr/convert_element_type | solution.py:106
  624.0 12.2 %fusion.133 = f32[2,1024,9,16]{1,3,2,0:T(8,128)} fusion(f32[2,1024,9,16]{1,3,2,0:T(8,128)} %get-tuple-element.310, s32[]{:T(128)S(6)} %copy.162, bf16[9,1024,1024]{1,2,0:T(8,128)(2,1)} %multiply_convert_fusion.12, bf16[2,1024,9,16]{1,3,2,0:T(8,128)(2,1)S(1)} %get-tuple-element.323), kind=kOutput, calls=%fused_computation.39.clone.1 | convolution fusion | flops 302137344 | bytes 19760128 | tf_op jit(solution)/shard_map/while/body/eval_jaxpr/hqk,qhd->khd/dot_general | solution.py:112
  636.2 9.8 %fusion.132 = f32[2,1024,9,16]{1,3,2,0:T(8,128)} fusion(f32[2,1024,9,16]{1,3,2,0:T(8,128)} %get-tuple-element.309, s32[]{:T(128)S(6)} %copy.162, bf16[9,1024,1024]{1,2,0:T(8,128)(2,1)} %multiply_convert_fusion.12, bf16[2,1024,9,16]{1,3,2,0:T(8,128)(2,1)S(1)} %get-tuple-element.322), kind=kOutput, calls=%fused_computation.37.clone.1 | convolution fusion | flops 302137344 | bytes 19760128 | tf_op jit(solution)/shard_map/while/body/eval_jaxpr/hqk,khd->qhd/dot_general | solution.py:108
  646.0 2.1 add_convert_fusion.2
  652.8 2.2 reshape.258
  657.8 1.8 add_convert_fusion
  660.2 64.2 %all-reduce.9 = (f32[13824]{0:T(1024)S(1)}, f32[2,144]{1,0:T(2,128)S(1)}, f32[8]{0:T(128)S(1)}, f32[8]{0:T(128)S(1)}) all-reduce(f32[13824]{0:T(1024)S(1)} %reshape.254, f32[2,144]{1,0:T(2,128)S(1)} %pad_maximum_fusion.12, f32[8]{0:T(128)S(1)} %copy-done.42, f32[8]{0:T(128)S(1)} %copy-done.41), channel_id=2, replica_groups=mesh['dp'=16,'fsdp'=8] {'dp','fsdp'}, use_global_device_ids=true, to_apply=%region_12.13.clone | all-reduce | flops 14128 | bytes 113024
  727.1 2.9 fusion.64
  730.1 140.4 %all-reduce.17.cloned.1.call-done = (f32[62208]{0:T(1024)}, f32[20736]{0:T(1024)}, f32[147456]{0:T(1024)}, f32[73728]{0:T(1024)}) async-done(((f32[62208]{0:T(1024)}, f32[20736]{0:T(1024)}, f32[147456]{0:T(1024)}, f32[73728]{0:T(1024)}), (f32[62208]{0:T(1024)}, f32[20736]{0:T(1024)}, f32[147456]{0:T(1024)}, f32[73728]{0:T(1024)})) %all-reduce.17.cloned.1.call-update) | async-done | bytes 1216528
  (188 shorter events, 47.9 us)
Async XLA Ops:
  7.2 71.8 %copy-start.43 = (s32[2,12]{1,0:T(2,128)S(1)}, s32[2,12]{1,0:T(2,128)}, u32[]{:S(2)}) copy-start(s32[2,12]{1,0:T(2,128)} %param.21) | copy-start | bytes 292
  7.2 151.6 %copy-start.25 = (bf16[2,1024,96]{1,2,0:T(8,128)(2,1)S(1)}, bf16[2,1024,96]{1,2,0:T(8,128)(2,1)}, u32[]{:S(2)}) copy-start(bf16[2,1024,96]{1,2,0:T(8,128)(2,1)} %param.18) | copy-start | bytes 1179652
  7.2 147.7 %all-reduce.19.cloned.1.call-start = ((), (), s32[]{:S(2)}) async-start(), calls=%async_computation.1 | async-start | bytes 143360
  9.7 290.0 %all-reduce.21.cloned.1.call-start = ((), (), s32[]{:S(2)}) async-start(), calls=%async_computation.2 | async-start | bytes 544768
  12.2 858.3 %all-reduce.17.cloned.1.call-start = ((), (), s32[]{:S(2)}) async-start(), calls=%async_computation | async-start | bytes 2441216
  35.7 265.2 %copy-start.39 = (f32[1,144]{1,0:T(1,128)}, f32[1,144]{1,0:T(1,128)S(1)}, u32[]{:S(2)}) copy-start(f32[1,144]{1,0:T(1,128)S(1)} %get-tuple-element.168) | copy-start | bytes 1732
  79.1 220.6 %copy-start.37 = (f32[2,96]{1,0:T(2,128)}, f32[2,96]{1,0:T(2,128)S(1)}, u32[]{:S(2)}) copy-start(f32[2,96]{1,0:T(2,128)S(1)} %pad_maximum_fusion.13) | copy-start | bytes 2308
  79.3 225.3 %copy-start.27 = (f32[1024,8]{0,1:T(8,128)}, f32[1024,8]{0,1:T(8,128)S(1)}, u32[]{:S(2)}) copy-start(f32[1024,8]{0,1:T(8,128)S(1)} %get-tuple-element.165) | copy-start | bytes 98308
  79.3 225.3 %copy-start.28 = (f32[1024,8]{0,1:T(8,128)}, f32[1024,8]{0,1:T(8,128)S(1)}, u32[]{:S(2)}) copy-start(f32[1024,8]{0,1:T(8,128)S(1)} %get-tuple-element.166) | copy-start | bytes 98308
  158.8 140.9 %copy-start.23 = (bf16[96,144]{1,0:T(8,128)(2,1)}, bf16[96,144]{1,0:T(8,128)(2,1)S(1)}, u32[]{:S(2)}) copy-start(bf16[96,144]{1,0:T(8,128)(2,1)S(1)} %reshape.242) | copy-start | bytes 82948
  159.3 142.4 %copy-start.4 = (f32[2,1024,144]{1,2,0:T(8,128)}, f32[2,1024,144]{1,2,0:T(8,128)S(1)}, u32[]{:S(2)}) copy-start(f32[2,1024,144]{1,2,0:T(8,128)S(1)} %get-tuple-element.170) | copy-start | bytes 3538948
  159.3 142.4 %copy-start.34 = (f32[2,1024]{1,0:T(2,128)}, f32[2,1024]{1,0:T(2,128)S(1)}, u32[]{:S(2)}) copy-start(f32[2,1024]{1,0:T(2,128)S(1)} %add_rsqrt_fusion.1) | copy-start | bytes 24580
  306.0 97.1 %copy-start.5 = (f32[2,1024,144]{1,2,0:T(8,128)S(1)}, f32[2,1024,144]{1,2,0:T(8,128)}, u32[]{:S(2)}) copy-start(f32[2,1024,144]{1,2,0:T(8,128)} %copy-done.4) | copy-start | bytes 3538948
  306.0 97.1 %copy-start.30 = (bf16[144,144]{1,0:T(8,128)(2,1)S(1)}, bf16[144,144]{1,0:T(8,128)(2,1)}, u32[]{:S(2)}) copy-start(bf16[144,144]{1,0:T(8,128)(2,1)} %reshape.247) | copy-start | bytes 124420
  403.5 9.6 %copy-start = (f32[2,1024,144]{1,2,0:T(8,128)}, f32[2,1024,144]{1,2,0:T(8,128)S(1)}, u32[]{:S(2)}) copy-start(f32[2,1024,144]{1,2,0:T(8,128)S(1)} %get-tuple-element.172) | copy-start | bytes 3538948
  441.2 15.5 %copy-start.7 = (bf16[2,1024,9,16]{1,3,2,0:T(8,128)(2,1)S(1)}, bf16[2,1024,9,16]{1,3,2,0:T(8,128)(2,1)}, u32[]{:S(2)}) copy-start(bf16[2,1024,9,16]{1,3,2,0:T(8,128)(2,1)} %get-tuple-element.326) | copy-start | bytes 1769476 | tf_op jit(solution)/shard_map/while
  526.1 9.8 %copy-start.14 = (f32[2,9,1024,1]{2,1,3,0:T(8,128)S(1)}, f32[2,9,1024,1]{2,1,3,0:T(8,128)}, u32[]{:S(2)}) copy-start(f32[2,9,1024,1]{2,1,3,0:T(8,128)} %copy-done.13) | copy-start | bytes 221188 | tf_op jit(solution)/shard_map/while
  551.3 15.5 %copy-start.7 = (bf16[2,1024,9,16]{1,3,2,0:T(8,128)(2,1)S(1)}, bf16[2,1024,9,16]{1,3,2,0:T(8,128)(2,1)}, u32[]{:S(2)}) copy-start(bf16[2,1024,9,16]{1,3,2,0:T(8,128)(2,1)} %get-tuple-element.326) | copy-start | bytes 1769476 | tf_op jit(solution)/shard_map/while
  636.2 9.8 %copy-start.14 = (f32[2,9,1024,1]{2,1,3,0:T(8,128)S(1)}, f32[2,9,1024,1]{2,1,3,0:T(8,128)}, u32[]{:S(2)}) copy-start(f32[2,9,1024,1]{2,1,3,0:T(8,128)} %copy-done.13) | copy-start | bytes 221188 | tf_op jit(solution)/shard_map/while
  646.0 2.2 copy-start.35
  646.0 2.3 copy-start.40
  646.0 2.2 copy-start.46
  651.3 3.7 copy-start.19
  651.3 4.7 copy-start.21
  652.8 4.9 copy-start.3
  657.7 2.4 copy-start.44
  657.8 2.4 copy-start.41
  657.8 2.4 copy-start.42
  657.8 66.6 %copy-start.45 = (f32[8]{0:T(128)S(1)}, f32[8]{0:T(128)}, u32[]{:S(2)}) copy-start(f32[8]{0:T(128)} %param.30) | copy-start | bytes 100
  659.6 66.5 %copy-start.24 = (bf16[96,144]{1,0:T(8,128)(2,1)S(1)}, bf16[96,144]{1,0:T(8,128)(2,1)}, u32[]{:S(2)}) copy-start(bf16[96,144]{1,0:T(8,128)(2,1)} %copy-done.23) | copy-start | bytes 82948
  659.6 67.5 %copy-start.1 = (f32[2,1024,144]{1,2,0:T(8,128)S(1)}, f32[2,1024,144]{1,2,0:T(8,128)}, u32[]{:S(2)}) copy-start(f32[2,1024,144]{1,2,0:T(8,128)} %copy-done) | copy-start | bytes 3538948
  659.6 67.5 %copy-start.12 = (bf16[512,144]{1,0:T(8,128)(2,1)S(1)}, bf16[512,144]{1,0:T(8,128)(2,1)}, u32[]{:S(2)}) copy-start(bf16[512,144]{1,0:T(8,128)(2,1)} %reshape.249) | copy-start | bytes 442372
  (21 other events, 25.0 us)
Sparse Core Ops, SparseCore 0:
  13.0 141.7 all-reduce.18
  160.6 139.0 all-reduce.20
  725.0 145.4 all-reduce.16
where the time goes:
time: 885 us; the launch traced here: 883 us
  waiting for transfers between devices  356 us (40%)
  matrix products  239 us (27%)
  blocking collectives  123 us (14%)
  other arithmetic  108 us (12%)
  local copies, waits for them, and re-layouts  30.1 us (3%)
  between operations  14.6 us (2%)
  loops' own time  11.3 us (1%)
    unnamed x6, waiting for transfers between devices  356 us
    unnamed x1, blocking collectives  64.2 us
    convert_element_type x2, other arithmetic, attend_back(): grad_scores = (chance * (grad_chance - jnp.sum(chance * grad_chance, axis...  62.7 us
    dot_general x4, matrix products, masked_scores(): jnp.einsum('qhd,khd->hqk', query, keys, preferred_element_type=jnp.float32)  59.8 us
    dot_general x2, matrix products, attend_back(): jnp.einsum('qhd,khd->hqk', grad_mixed, values, preferred_element_type=jnp...  51.7 us
    all_gather x1, blocking collectives, body(): lax.all_gather(w_gu, ('dp', 'fsdp'), axis=0, tiled=True)  40.4 us
    reduce_sum x2, other arithmetic, attend_series(): total = jax.nn.logsumexp(scores, axis=-1, keepdims=True)  33.2 us
    dot_general x2, matrix products, attend_series(): jnp.einsum('hqk,khd->qhd', weights, values, preferred_element_type=jnp.fl...  32.4 us
  transfers between devices with their start and end apart: 3, of which 3 were waited for; matrix products, arithmetic and copies ran while one was open for 2% of the time, Pallas kernels for 0%

commit v1 on v0

v1 whole, which is shorter than its diff:
```python
import functools
import jax
import jax.numpy as jnp
import numpy as np
from jax import lax
from jax.experimental import pallas as pl
from jax.experimental.pallas import tpu as pltpu

D, H, HD, FF, NDATE, F, NSET, LEN = 144, 9, 16, 512, 12, 96, 8, 1024
EPS = 1e-05
TOK = 256
QT = 256
f32, bf16 = jnp.float32, jnp.bfloat16


def dot(a, b, ca=1, cb=0):
    return lax.dot_general(a, b, (((ca,), (cb,)), ((), ())), preferred_element_type=f32)


def rope_tables():
    freqs = np.float32(10000.0) ** (-np.arange(HD // 2, dtype=np.float32) * np.float32(2.0) / np.float32(HD))
    angle = np.arange(LEN, dtype=np.float32)[None, :] * freqs.astype(np.float32)[:, None]
    return np.cos(angle.astype(np.float64)).astype(np.float32), np.sin(angle.astype(np.float64)).astype(np.float32)


def main_kernel(feats, dout, fac, gains, cosr, sinr, win, wqkv, wout, wgu, wdown,
                out, gfeats, g_in, g_qkv, g_out, g_gu, g_down, g_gain,
                winT, wqkvT, woutT, wguT, wdownT,
                lifted, first, inv1, normed, q, k, v, prob, rl, osum, mixed, second, hidden, both,
                gmid, gbranch, gmixed, gjoint, gfirst):
    s = pl.program_id(0)

    @pl.when(s == 0)
    def _():
        for src, dst in ((win, winT), (wqkv, wqkvT), (wout, woutT), (wgu, wguT), (wdown, wdownT)):
            dst[...] = src[...].astype(f32).T.astype(bf16)
        for ref in (g_in, g_qkv, g_out, g_gu, g_down, g_gain):
            ref[...] = jnp.zeros_like(ref)

    gain0 = gains[:, 0:1]
    gain1 = gains[:, 1:2]
    factor = fac[0]

    @pl.loop(0, LEN // TOK)
    def _(i):
        t = pl.ds(pl.multiple_of(i * TOK, TOK), TOK)
        lift = (feats[0, :, t].astype(f32) * factor).astype(bf16)
        lifted[:, t] = lift
        x = dot(winT[...], lift)
        first[:, t] = x
        r = lax.rsqrt(jnp.mean(x * x, axis=0, keepdims=True) + EPS)
        inv1[:, t] = r
        n = (x * r * gain0).astype(bf16)
        normed[:, t] = n
        joint = dot(wqkvT[...], n).reshape(3, H, HD, TOK)
        c, sn = cosr[:, t][None], sinr[:, t][None]
        for which, ref, scale in ((0, q, 0.25), (1, k, 1.0)):
            a, b = joint[which, :, :8], joint[which, :, 8:]
            ref[:, :, t] = (jnp.concatenate([a * c - b * sn, b * c + a * sn], axis=1) * scale).astype(bf16)
        v[:, :, t] = joint[2].astype(bf16)

    diag = lax.broadcasted_iota(jnp.int32, (QT, QT), 0) <= lax.broadcasted_iota(jnp.int32, (QT, QT), 1)

    @pl.loop(0, H)
    def _(h):
        kt = k[h].astype(f32).T.astype(bf16)
        vh = v[h]
        for j in range(LEN // QT):
            n = (j + 1) * QT
            cols = pl.ds(j * QT, QT)
            sc = dot(kt[:n], q[h, :, cols])
            last = jnp.where(diag, sc[n - QT:], -1e30)
            top = jnp.max(last, axis=0, keepdims=True)
            if j:
                top = jnp.maximum(top, jnp.max(sc[:n - QT], axis=0, keepdims=True))
                p0 = jnp.exp(sc[:n - QT] - top)
            p1 = jnp.exp(last - top)
            total = jnp.sum(p1, axis=0, keepdims=True)
            if j:
                total = total + jnp.sum(p0, axis=0, keepdims=True)
                prob[h, : n - QT, cols] = p0.astype(bf16)
            prob[h, n - QT : n, cols] = p1.astype(bf16)
            o = dot(vh[:, :n], prob[h, :n, cols])
            inv = 1.0 / total
            rl[h, :, cols] = inv
            o = o * inv
            osum[h, :, cols] = o
            mixed[h, :, cols] = o.astype(bf16)

    @pl.loop(0, LEN // TOK)
    def _(i):
        t = pl.ds(pl.multiple_of(i * TOK, TOK), TOK)
        mid = first[:, t] + dot(woutT[...], mixed[:, :, t].reshape(D, TOK))
        r = lax.rsqrt(jnp.mean(mid * mid, axis=0, keepdims=True) + EPS)
        sec = (mid * r * gain1).astype(bf16)
        second[:, t] = sec
        g = dout[0, :, t]
        C = 128
        for f in range(0, FF, C):
            gate = dot(wguT[f : f + C], sec)
            up = dot(wguT[FF + f : FF + f + C], sec)
            gh = dot(wdown[f : f + C], g)
            sig = 1.0 / (1.0 + jnp.exp(-gate))
            silu = gate * sig
            hidden[f : f + C, t] = (silu * up).astype(bf16)
            both[FF + f : FF + f + C, t] = (gh * silu).astype(bf16)
            both[f : f + C, t] = (gh * up * (sig + silu * (1.0 - sig))).astype(bf16)
        out[0, :, t] = (mid + dot(wdownT[...], hidden[:, t])).astype(bf16)
        c = dot(wgu[...], both[:, t])
        cg = c * gain1
        inner = jnp.mean(cg * mid, axis=0, keepdims=True)
        gain_part = c * mid * r
        g_gain[1] += gain_part[:, :128] + gain_part[:, 128:]
        gm = g.astype(f32) + r * cg - mid * (r * r * r * inner)
        gmid[:, t] = gm
        gb = gm.astype(bf16)
        gbranch[:, t] = gb
        gmixed[:, :, t] = dot(wout[...], gb).reshape(H, HD, TOK)

    g_down[...] += dot(hidden[...], dout[0], 1, 1)
    g_gu[...] += dot(second[...], both[...], 1, 1)
    g_out[...] += dot(mixed[...].reshape(D, LEN), gbranch[...], 1, 1)

    @pl.loop(0, H)
    def _(h):
        do = (gmixed[h] * rl[h]).astype(bf16)
        delta = jnp.sum(do.astype(f32) * osum[h], axis=0, keepdims=True)
        vt = v[h].astype(f32).T.astype(bf16)
        kh = k[h]
        dk = jnp.zeros((HD, LEN), f32)
        dv = jnp.zeros((HD, LEN), f32)
        dqs = []
        for j in range(LEN // QT):
            n = (j + 1) * QT
            cols = slice(j * QT, n)
            dp = dot(vt[:n], do[:, cols])
            p = prob[h, :n, cols]
            ds = (p.astype(f32) * (dp - delta[:, cols])).astype(bf16)
            dqs.append(dot(kh[:, :n], ds))
            pad = lambda a: a if n == LEN else jnp.concatenate([a, jnp.zeros((HD, LEN - n), f32)], axis=1)
            dk += pad(dot(q[h, :, cols], ds, 1, 1))
            dv += pad(dot(do[:, cols], p, 1, 1))
        dq = jnp.concatenate(dqs, axis=1) * 0.25
        c, sn = cosr[...], sinr[...]
        for which, val in ((0, dq), (1, dk)):
            a, b = val[:8], val[8:]
            gjoint[which, h] = jnp.concatenate([a * c + b * sn, b * c - a * sn], axis=0).astype(bf16)
        gjoint[2, h] = dv.astype(bf16)

    @pl.loop(0, LEN // TOK)
    def _(i):
        t = pl.ds(pl.multiple_of(i * TOK, TOK), TOK)
        c = dot(wqkv[...], gjoint[:, :, :, t].reshape(3 * D, TOK))
        x, r = first[:, t], inv1[:, t]
        cg = c * gain0
        inner = jnp.mean(cg * x, axis=0, keepdims=True)
        gain_part = c * x * r
        g_gain[0] += gain_part[:, :128] + gain_part[:, 128:]
        gf = (gmid[:, t] + r * cg - x * (r * r * r * inner)).astype(bf16)
        gfirst[:, t] = gf
        gfeats[0, :, t] = (dot(win[...], gf) * factor).astype(bf16)

    g_qkv[...] += dot(normed[...], gjoint[...].reshape(3 * D, LEN), 1, 1)
    g_in[...] += dot(lifted[...], gfirst[...], 1, 1)


def run_main(feats_t, dout_t, fac, gains_t, mats):
    cos, sin = rope_tables()
    S = feats_t.shape[0]
    full = lambda *shape: pl.BlockSpec(shape, lambda s: (0,) * len(shape))
    per = lambda *shape: pl.BlockSpec((1,) + shape, lambda s: (s,) + (0,) * len(shape))
    sd = jax.ShapeDtypeStruct
    V = pltpu.VMEM
    return pl.pallas_call(
        main_kernel,
        grid=(S,),
        in_specs=[per(F, LEN), per(D, LEN), per(F, 1), full(D, 2), full(8, LEN), full(8, LEN),
                  full(F, D), full(D, 3 * D), full(D, D), full(D, 2 * FF), full(FF, D)],
        out_specs=[per(D, LEN), per(F, LEN), full(F, D), full(D, 3 * D), full(D, D), full(D, 2 * FF), full(FF, D),
                   full(2, D, 128)],
        out_shape=[sd((S, D, LEN), bf16), sd((S, F, LEN), bf16), sd((F, D), f32), sd((D, 3 * D), f32), sd((D, D), f32),
                   sd((D, 2 * FF), f32), sd((FF, D), f32), sd((2, D, 128), f32)],
        scratch_shapes=[
            V((D, F), bf16), V((3 * D, D), bf16), V((D, D), bf16), V((2 * FF, D), bf16), V((D, FF), bf16),
            V((F, LEN), bf16), V((D, LEN), f32), V((1, LEN), f32), V((D, LEN), bf16),
            V((H, HD, LEN), bf16), V((H, HD, LEN), bf16), V((H, HD, LEN), bf16),
            V((H, LEN, LEN), bf16), V((H, 1, LEN), f32), V((H, HD, LEN), f32), V((H, HD, LEN), bf16),
            V((D, LEN), bf16), V((FF, LEN), bf16), V((2 * FF, LEN), bf16),
            V((D, LEN), f32), V((D, LEN), bf16), V((H, HD, LEN), f32), V((3, H, HD, LEN), bf16), V((D, LEN), bf16),
        ],
        compiler_params=pltpu.CompilerParams(vmem_limit_bytes=60 * 2**20, dimension_semantics=("arbitrary",)),
    )(feats_t, dout_t, fac, gains_t, jnp.asarray(cos), jnp.asarray(sin), *mats)


SIZES = (108, 486, 162, 1152, 576)
SHAPES = ((F, D), (D, 3 * D), (D, D), (D, 2 * FF), (FF, D))
BOTH = ("dp", "fsdp")


def body(feats, targets, lag_mask, date_mask, freq_ids, dataset_ids, w_in, w_qkv, w_out, w_gu, w_down, gains, running, d_out):
    packed = jnp.concatenate([w_in, w_qkv, w_out, w_gu, w_down, gains.reshape(-1)])
    gathered = lax.all_gather(packed, BOTH, axis=0, tiled=False)
    mats, at = [], 0
    for size, shape in zip(SIZES, SHAPES):
        mats.append(gathered[:, at : at + size].reshape(shape))
        at += size
    gain_full = gathered[::8, at:].reshape(16, 2, 9).transpose(1, 0, 2).reshape(2, D).astype(f32)
    scale = jnp.mean(jnp.abs(targets), axis=1) + 1e-5
    keep = date_mask * (jnp.arange(NDATE, dtype=jnp.int32)[None, :] >= (freq_ids * (NDATE // 3))[:, None]).astype(jnp.int32)
    fac = jnp.concatenate([lag_mask.astype(f32) / scale[:, None], keep.astype(f32)], axis=1)
    member = (dataset_ids[:, None] == jnp.arange(NSET, dtype=jnp.int32)[None, :]).astype(f32)
    stats = jnp.concatenate([jnp.sum(member * scale[:, None], axis=0), jnp.sum(member, axis=0)])
    res = run_main(jnp.swapaxes(feats, 1, 2), jnp.swapaxes(d_out, 1, 2), fac[:, :, None], gain_full.T, mats)
    gain_grad = res[7].sum(-1).reshape(2, 16, 9).transpose(1, 0, 2).reshape(16, 1, 18)
    parts = [g.reshape(128, size) for g, size in zip(res[2:7], SIZES)]
    parts += [jnp.broadcast_to(gain_grad, (16, 8, 18)).reshape(128, 18), jnp.broadcast_to(stats[None], (128, 16))]
    own = lax.psum_scatter(jnp.concatenate(parts, axis=1), BOTH, scatter_dimension=0, tiled=True).reshape(-1)
    outs, at = [], 0
    for size in SIZES:
        outs.append(own[at : at + size])
        at += size
    grad_gains = own[at : at + 18].reshape(2, 9)
    set_sums, set_counts = own[at + 18 : at + 26], own[at + 26 : at + 34]
    batch_mean = set_sums / jnp.maximum(set_counts, 1.0)
    running_next = jnp.where(set_counts > 0.5, 0.75 * running + 0.25 * batch_mean, running)
    return (jnp.swapaxes(res[0], 1, 2), jnp.swapaxes(res[1], 1, 2), *outs, grad_gains, running_next)


def solution(mesh):
    P = jax.sharding.PartitionSpec
    flat, rows, cube = P(BOTH), P(BOTH, None), P(BOTH, None, None)
    return jax.shard_map(
        body,
        mesh=mesh,
        in_specs=(cube, rows, rows, rows, flat, flat, flat, flat, flat, flat, flat, P(None, "dp"), P(), cube),
        out_specs=(cube, cube, flat, flat, flat, flat, flat, P(None, "dp"), P()),
        check_vma=False,
    )
```

time: 885 us -> 429 us (0.48)
  matrix products: 239 us -> 0 us
  blocking collectives: 123 us -> 0 us
  other arithmetic: 108 us -> 2.01 us
  Pallas kernels: 0 us -> 90.1 us
  waiting for transfers between devices: 356 us -> 294 us
  loops' own time: 11.3 us -> 0 us
    dot_general x29 -> x0, matrix products: 239 us -> none  [the longest x4 59.8 us: masked_scores(): jnp.einsum('qhd,khd->hqk', query, keys, preferred_element_type=jnp.float32)]
    pallas_call x0 -> x1, Pallas kernels: none -> 90.1 us  [run_main(): pl.pallas_call(main_kernel, grid=(S,), in_specs=[per(F, LEN), per(D, LEN)...]
    convert_element_type x5 -> x1, other arithmetic: 64.5 us -> 0.07 us  [body(): keep.astype(f32)]
    unnamed x1 -> x0, blocking collectives: 64.2 us -> none
    unnamed x6 -> x4, waiting for transfers between devices: 356 us -> 294 us
    all_gather x2 -> x0, blocking collectives: 58.7 us -> none  [the longest x1 40.4 us: body(): lax.all_gather(w_gu, ('dp', 'fsdp'), axis=0, tiled=True)]
    reduce_sum x4 -> x3, other arithmetic: 35.3 us -> 0.35 us  [the longest x1 0.15 us: body(): res[7].sum(-1).reshape(2, 16, 9).transpose(1, 0, 2).reshape(16, 1, 18)]
    unnamed x103 -> x22, local copies, waits for them, and re-layouts: 15.4 us -> 1.25 us
  transfers between devices with their start and end apart: 3 -> 2, of which waited for: 3 -> 2; matrix products, arithmetic and copies ran while one was open for 2% -> 0% of each run, Pallas kernels for 0% -> 0%
where the time goes in v1:
time: 429 us; the launch traced here: 428 us
  waiting for transfers between devices  294 us (69%)
  Pallas kernels  90.1 us (21%)
  local copies, waits for them, and re-layouts  27.9 us (7%)
  between operations  14.3 us (3%)
    unnamed x4, waiting for transfers between devices  294 us
    pallas_call x1, Pallas kernels, run_main(): pl.pallas_call(main_kernel, grid=(S,), in_specs=[per(F, LEN), per(D, LEN)...  90.1 us
  transfers between devices with their start and end apart: 2, of which 2 were waited for; matrix products, arithmetic and copies ran while one was open for 0% of the time, Pallas kernels for 0%

profile of v1, /device:TPU:1, one launch (start us, length us, event | category | flops | bytes accessed | tf_op | source)
XLA Modules:
  0.0 427.9 jit_solution(14740751653924144720)
XLA Ops:
  7.3 0.7 reshape.92
  8.0 3.5 concatenate.13
  11.6 0.3 dynamic-update-slice
  11.9 0.9 copy-done
  12.8 0.1 abs_reduce_fusion
  13.2 0.8 copy.36.fac
  14.1 147.7 %all-reduce.5.cloned.1.call-done = bf16[320256]{0:T(1024)(128)(2,1)} async-done(((bf16[320256]{0:T(1024)(128)(2,1)}), bf16[320256]{0:T(1024)(128)(2,1)}) %all-reduce.5.cloned.1.call-update) | async-done | bytes 640528
  161.8 2.0 reshape.108
  164.1 0.1 slice.82
  164.3 0.1 slice.83
  164.6 0.7 copy.35
  165.3 0.7 reshape.93.win
  166.0 0.9 reshape.94.wqkv
  166.9 0.8 reshape.95.wout
  167.7 1.0 reshape.96.wgu
  168.8 0.9 reshape.97.wdown
  169.7 90.1 %shard_map.223 = (bf16[2,144,1024]{2,1,0:T(8,128)(2,1)}, bf16[2,96,1024]{2,1,0:T(8,128)(2,1)}, f32[96,144]{1,0:T(8,128)}, f32[144,432]{1,0:T(8,128)}, f32[144,14...) custom-call(bf16[2,96,1024]{2,1,0:T(8,128)(2,1)} %bitcast.22, ...), custom_call_target="tpu_custom_call" | custom-call | tf_op jit(solution)/shard_map/pallas_call | solution.py:174
  259.8 1.1 reshape.98
  260.9 1.4 reshape.99
  262.3 1.1 reshape.100
  263.5 0.3 reshape.102
  263.8 0.1 reduce_sum.37
  264.1 1.5 concatenate.15
  265.7 145.9 %all-reduce.7.cloned.1.call-done = f32[128,2518]{1,0:T(8,128)} async-done(((f32[128,2518]{1,0:T(8,128)}), f32[128,2518]{1,0:T(8,128)}) %all-reduce.7.cloned.1.call-update) | async-done | bytes 1289232
  411.5 0.8 dynamic-slice_reduce_fusion.2
  412.3 0.6 reshape.105
  412.9 1.2 dynamic-slice_bitcast_fusion
  414.1 1.4 dynamic-slice.2
  415.5 1.3 dynamic-slice.3
  416.9 1.5 dynamic-slice_reduce_fusion
  418.3 1.4 dynamic-slice_reduce_fusion.1
  419.7 1.3 bitcast_select_fusion
  (44 shorter events, 1.4 us)
Async XLA Ops:
  7.2 5.6 %copy-start.9 = (s32[2]{0:T(128)S(1)}, s32[2]{0:T(128)}, u32[]{:S(2)}) copy-start(s32[2]{0:T(128)} %param.20) | copy-start | bytes 28
  7.2 5.6 %copy-start.4 = (f32[2,1024]{1,0:T(2,128)S(1)}, f32[2,1024]{1,0:T(2,128)}, u32[]{:S(2)}) copy-start(f32[2,1024]{1,0:T(2,128)} %param.17) | copy-start | bytes 24580
  7.2 5.8 %copy-start.5 = (s32[2,12]{1,0:T(2,128)S(1)}, s32[2,12]{1,0:T(2,128)}, u32[]{:S(2)}) copy-start(s32[2,12]{1,0:T(2,128)} %param.19) | copy-start | bytes 292
  7.2 5.8 %copy-start.6 = (s32[2,84]{1,0:T(2,128)S(1)}, s32[2,84]{1,0:T(2,128)}, u32[]{:S(2)}) copy-start(s32[2,84]{1,0:T(2,128)} %param.18) | copy-start | bytes 2020
  7.2 6.7 %copy-start.8 = (s32[2]{0:T(128)S(1)}, s32[2]{0:T(128)}, u32[]{:S(2)}) copy-start(s32[2]{0:T(128)} %param.21) | copy-start | bytes 28
  7.2 154.6 %all-reduce.5.cloned.1.call-start = ((), (), s32[]{:S(2)}) async-start(), calls=%async_computation | async-start | bytes 1282048
  11.9 0.9 copy-start
  12.7 398.8 %all-reduce.7.cloned.1.call-start = ((), (), s32[]{:S(2)}) async-start(), calls=%async_computation.1 | async-start | bytes 2621440
  259.8 3.6 copy-start.1
  259.8 3.7 copy-start.2
  260.9 2.9 copy-start.3
  265.6 154.1 %copy-start.7 = (f32[8]{0:T(128)S(1)}, f32[8]{0:T(128)}, u32[]{:S(2)}) copy-start(f32[8]{0:T(128)} %param.28) | copy-start | bytes 100
Sparse Core Ops, SparseCore 0:
  12.9 148.9 all-reduce.4
  265.8 145.7 all-reduce.6

commit v2 on v1

v2 whole, which is shorter than its diff:
```python
import functools

import jax
import jax.numpy as jnp
import numpy as np
from jax import lax
from jax.experimental import pallas as pl
from jax.experimental.pallas import tpu as pltpu
from jax.sharding import PartitionSpec as P

D, H, HD, FF, NDATE, NLAG, F, NSET, LEN = 144, 9, 16, 512, 12, 84, 96, 8, 1024
EPS = 1e-05
TOK = 256
QT = 256
CH = 128
f32, bf16 = jnp.float32, jnp.bfloat16
MESH = pl.DeviceIdType.MESH
BOTH = ("dp", "fsdp")

A_ROWS, B_ROWS = 8, 16
SPECS = {
    "in": (D, 108, 4, 3, "a", 0),
    "qkv": (3 * D, 486, 8, 9, "a", 1),
    "gu": (2 * FF, 1152, 8, 9, "b", 0),
    "down": (D, 576, 2, 8, "b", 9),
    "out": (D, 162, 8, 9, "b", 14),
}
ROWS = {"in": F, "qkv": D, "gu": D, "down": FF, "out": D}


def dot(a, b, ca=1, cb=0, **kw):
    return lax.dot_general(a, b, (((ca,), (cb,)), ((), ())), preferred_element_type=f32, **kw)


def lane_tiles(width):
    return [(t // 128, t, min(128, width - t)) for t in range(0, width, 128)]


def pieces(piece, source, count):
    cuts = []
    for i in range(count):
        at, left, parts = i * piece, piece, []
        while left:
            c, o = divmod(at, source)
            n = min(left, source - o)
            parts.append((c, o, n))
            at, left = at + n, left - n
        cuts.append(parts)
    return cuts


def spot(c):
    return (c % 2) * 64 + c // 2


def join(parts):
    return parts[0] if len(parts) == 1 else jnp.concatenate(parts, axis=1)


def unpack(flat, rows, name, dst):
    cols, chunk, gc, gr, _, base = SPECS[name]
    groups, kept = 128 // gc, {}

    def owner(c):
        if c not in kept:
            kept[c] = join(
                [flat[pl.ds(spot(c) * rows + base + t, groups, stride=gc // 2 * rows), :] for t, _, _ in lane_tiles(chunk)]
            )
        return kept[c]

    for i, parts in enumerate(pieces(cols, chunk, gr)):
        row = join([owner(c)[:, o : o + n] for c, o, n in parts])
        for t, at, width in lane_tiles(cols):
            dst[t, pl.ds(i, groups, stride=gr), :width] = row[:, at : at + width]


def pack(src, name, flat, rows):
    cols, chunk, gc, gr, _, base = SPECS[name]
    groups, kept = 128 // gc, {}

    def line(i):
        if i not in kept:
            kept[i] = join([src[t, pl.ds(i, groups, stride=gr), :] for t, _, _ in lane_tiles(cols)])
        return kept[i]

    for c, parts in enumerate(pieces(chunk, cols, gc)):
        run = [line(i)[:, o : o + n] for i, o, n in parts]
        run = join(run + ([jnp.zeros((groups, -chunk % 128), f32)] if chunk % 128 else []))
        for t, at, _ in lane_tiles(chunk):
            flat[pl.ds(spot(c) * rows + base + t, groups, stride=gc // 2 * rows), :] = run[:, at : at + 128]


def place():
    fs = lax.axis_index("fsdp")
    return lax.axis_index("dp"), fs // 2, fs % 2


def partners():
    dp, y, core = place()
    across = lambda o: (lax.rem(dp + o, 16), 2 * y + core)
    along = lambda o: (dp, 2 * lax.rem(y + o, 4) + core)
    return across, along, (dp, 2 * y + 1 - core)


def enter():
    across, along, sibling = partners()
    barrier = pltpu.get_barrier_semaphore()

    @pl.loop(1, 16)
    def _(o):
        pl.semaphore_signal(barrier, inc=1, device_id=across(o), device_id_type=MESH)

    for o in (1, 2, 3):
        pl.semaphore_signal(barrier, inc=1, device_id=along(o), device_id_type=MESH)
    pl.semaphore_signal(barrier, inc=1, device_id=sibling, device_id_type=MESH)
    pl.semaphore_wait(barrier, 19)


def send(src, dst, sems, k, to):
    pltpu.make_async_remote_copy(
        src_ref=src, dst_ref=dst, send_sem=sems.at[0, k], recv_sem=sems.at[1, k], device_id=to, device_id_type=MESH
    ).start()


def wait(ref, sem):
    pltpu.make_async_copy(ref, ref, sem).wait()


class Gather:
    def __init__(self, own, everyone, sems):
        self.own, self.all, self.sems = own, everyone, sems

    def first(self):
        dp, y, core = place()
        _, along, _ = partners()
        for o in (1, 2, 3):
            send(self.own, self.all.at[core, dp, y], self.sems, 0, along(o))
        self.all[core, dp, y] = self.own[...]

    def second(self):
        dp, y, core = place()
        across, _, _ = partners()
        wait(self.all.at[core, dp, pl.ds(0, 3)], self.sems.at[1, 0])
        wait(self.all.at[core, dp, pl.ds(0, 3)], self.sems.at[0, 0])
        line = self.all.at[core, dp]

        @pl.loop(1, 16)
        def _(o):
            send(line, line, self.sems, 1, across(o))

    def third(self):
        _, _, core = place()
        _, _, sibling = partners()
        wait(self.all.at[core, pl.ds(0, 15)], self.sems.at[1, 1])
        wait(self.all.at[core, pl.ds(0, 15)], self.sems.at[0, 1])
        send(self.all.at[core], self.all.at[core], self.sems, 2, sibling)

    def last(self):
        _, _, core = place()
        wait(self.all.at[core], self.sems.at[1, 2])
        wait(self.all.at[core], self.sems.at[0, 2])


class Reduce:
    def __init__(self, parts, half, row, line, sems):
        self.parts, self.half, self.row, self.line, self.sems = parts, half, row, line, sems

    def first(self):
        _, _, core = place()
        _, _, sibling = partners()
        send(self.parts.at[1 - core], self.half, self.sems, 0, sibling)

    def second(self):
        dp, y, core = place()
        across, _, _ = partners()
        wait(self.half, self.sems.at[1, 0])
        wait(self.half, self.sems.at[0, 0])
        self.half[...] = (self.half[...].astype(f32) + self.parts[core].astype(f32)).astype(self.half.dtype)

        @pl.loop(1, 16)
        def _(o):
            send(self.half.at[lax.rem(dp + o, 16)], self.row.at[dp], self.sems, 1, across(o))

        self.row[dp] = self.half[dp]

    def third(self):
        dp, y, core = place()
        _, along, _ = partners()
        wait(self.row.at[pl.ds(0, 15)], self.sems.at[1, 1])
        wait(self.row.at[pl.ds(0, 15)], self.sems.at[0, 1])
        mine = jnp.sum(self.row[...].astype(f32), axis=0).astype(self.row.dtype)
        self.half[0] = mine
        for o in (1, 2, 3):
            send(self.half.at[0, lax.rem(y + o, 4)], self.line.at[y], self.sems, 2, along(o))
        self.line[y] = self.half[0, y]

    def last(self):
        wait(self.line.at[pl.ds(0, 3)], self.sems.at[1, 2])
        wait(self.line.at[pl.ds(0, 3)], self.sems.at[0, 2])
        return jnp.sum(self.line[...].astype(f32), axis=0)


def rope_tables():
    freqs = np.float32(10000.0) ** (-np.arange(HD // 2, dtype=np.float32) * np.float32(2.0) / np.float32(HD))
    angle = np.arange(LEN, dtype=np.float32)[None, :] * freqs.astype(np.float32)[:, None]
    return np.cos(angle.astype(np.float64)).astype(np.float32), np.sin(angle.astype(np.float64)).astype(np.float32)


def own_tiles(w_in, w_qkv, w_out, w_gu, w_down, gains, tile_a, tile_b, wide):
    tile_a[...] = jnp.zeros_like(tile_a)
    wide[...] = jnp.zeros_like(wide)
    for name, ref in (("in", w_in), ("qkv", w_qkv), ("out", w_out), ("gu", w_gu), ("down", w_down)):
        _, chunk, _, _, which, base = SPECS[name]
        for t, at, width in lane_tiles(chunk):
            (tile_a if which == "a" else wide)[base + t, :width] = ref[pl.ds(at, width)].astype(f32)
    tile_a[0:1, 108:117] = gains[0:1, :].astype(f32)
    tile_a[0:1, 117:126] = gains[1:2, :].astype(f32)
    tile_b[...] = wide[...].astype(bf16)


def gain_columns(flat, out):
    rows = flat[pl.ds(0, 16, stride=4 * A_ROWS), :]
    r = lax.broadcasted_iota(jnp.int32, (D, 16), 0) // 9
    spread = dot((r == lax.broadcasted_iota(jnp.int32, (D, 16), 1)).astype(f32), rows)
    lane = lax.broadcasted_iota(jnp.int32, (D, 128), 1)
    e = lax.rem(lax.broadcasted_iota(jnp.int32, (D, 128), 0), 9)
    for i in (0, 1):
        out[:, i : i + 1] = jnp.sum(jnp.where(lane == e + 108 + 9 * i, spread, 0.0), axis=1, keepdims=True)


def gain_rows(partial, flat):
    pos = lax.broadcasted_iota(jnp.int32, (128, D), 0)
    r = lax.broadcasted_iota(jnp.int32, (128, D), 1) // 9
    pick = (lax.rem(pos, 64) // 4 == r).astype(f32)
    lane = lax.broadcasted_iota(jnp.int32, (D, 128), 1)
    e = lax.rem(lax.broadcasted_iota(jnp.int32, (D, 128), 0), 9)
    cols = jnp.zeros((D, 128), f32)
    for i in (0, 1):
        cols += jnp.where(lane == e + 108 + 9 * i, jnp.sum(partial[i], axis=1, keepdims=True), 0.0)
    spread = dot(pick, cols, precision=lax.Precision.HIGHEST)
    flat[pl.ds(0, 128, stride=A_ROWS), :] += spread


def series_scalars(targets, lag_mask, date_mask, freq, sets, factor, stats):
    scale = jnp.sum(jnp.abs(targets[...]), axis=1, keepdims=True) / LEN + 1e-5
    lag = lag_mask[...].astype(f32) / scale
    second = lax.broadcasted_iota(jnp.int32, (2, NDATE), 0) == 1
    start = jnp.where(second, freq[1], freq[0]) * (NDATE // 3)
    keep = jnp.where(lax.broadcasted_iota(jnp.int32, (2, NDATE), 1) >= start, date_mask[...], 0).astype(f32)
    both = jnp.concatenate([lag, keep], axis=1)
    both = jnp.concatenate([both, jnp.zeros((2, 32), f32)], axis=1)
    both = jnp.concatenate([both, jnp.zeros((6, 128), f32)], axis=0)
    factor[...] = both.T
    lane = lax.broadcasted_iota(jnp.int32, (1, 128), 1)
    row = jnp.zeros((1, 128), f32)
    for s in (0, 1):
        row += jnp.where(lane == sets[s], scale[s : s + 1], 0.0) + jnp.where(lane == sets[s] + NSET, 1.0, 0.0)
    stats[...] = row


def gather_kernel(w_in, w_qkv, w_out, w_gu, w_down, gains, win, wqkv, wout, wgu, wdown, winT, wqkvT, woutT, wguT, wdownT, gain_cols,
                  tile_a, tile_b, wide, all_a, all_b, flat_a, flat_b, *rest):
    mats, (sem_a, sem_b) = rest[:5], rest[5:]
    own_tiles(w_in, w_qkv, w_out, w_gu, w_down, gains, tile_a, tile_b, wide)
    enter()
    a, b = Gather(tile_a, all_a, sem_a), Gather(tile_b, all_b, sem_b)
    a.first()
    b.first()
    a.second()
    b.second()
    a.third()
    b.third()
    a.last()
    flat_a[...] = all_a[...].reshape(128 * A_ROWS, 128)
    gain_columns(flat_a, gain_cols)

    def emit(name, flat, rows, mat, out, outT):
        unpack(flat, rows, name, mat)
        for t, at, width in lane_tiles(SPECS[name][0]):
            val = mat[t][:, :width]
            out[:, at : at + width] = val.astype(bf16)
            outT[at : at + width, :] = val.T.astype(bf16)

    emit("in", flat_a, A_ROWS, mats[0], win, winT)
    emit("qkv", flat_a, A_ROWS, mats[1], wqkv, wqkvT)
    b.last()
    flat_b[...] = all_b[...].astype(f32).reshape(128 * B_ROWS, 128)
    emit("out", flat_b, B_ROWS, mats[2], wout, woutT)
    emit("gu", flat_b, B_ROWS, mats[3], wgu, wguT)
    emit("down", flat_b, B_ROWS, mats[4], wdown, wdownT)


VM = pl.BlockSpec(memory_space=pltpu.VMEM)
SM = pl.BlockSpec(memory_space=pltpu.SMEM)


def tiled(name):
    return (-(-SPECS[name][0] // 128), ROWS[name], 128)


NAMES = ("in", "qkv", "out", "gu", "down")


def gather_all(w_in, w_qkv, w_out, w_gu, w_down, gains):
    sd, V = jax.ShapeDtypeStruct, pltpu.VMEM
    shapes = [(ROWS[n], SPECS[n][0]) for n in NAMES]
    return pl.pallas_call(
        gather_kernel,
        in_specs=[VM] * 6,
        out_specs=[VM] * 11,
        out_shape=[sd(s, bf16) for s in shapes] + [sd(s[::-1], bf16) for s in shapes] + [sd((D, 2), f32)],
        scratch_shapes=[V((A_ROWS, 128), f32), V((B_ROWS, 128), bf16), V((B_ROWS, 128), f32),
                        V((2, 16, 4, A_ROWS, 128), f32), V((2, 16, 4, B_ROWS, 128), bf16),
                        V((128 * A_ROWS, 128), f32), V((128 * B_ROWS, 128), f32)]
        + [V(tiled(n), f32) for n in NAMES]
        + [pltpu.SemaphoreType.DMA((2, 3))] * 2,
        compiler_params=pltpu.CompilerParams(collective_id=0, has_side_effects=True, vmem_limit_bytes=40 * 2**20),
    )(w_in, w_qkv, w_out, w_gu, w_down, gains)


def reduce_kernel(g_in, g_qkv, g_out, g_gu, g_down, g_gain, stats, running,
                  o_in, o_qkv, o_out, o_gu, o_down, o_gain, o_running,
                  flat_a, flat_b, parts_a, parts_b, half_a, half_b, row_a, row_b, line_a, line_b, total_b, sem_a, sem_b):
    flat_a[...] = jnp.zeros_like(flat_a)
    flat_b[...] = jnp.zeros_like(flat_b)
    pack(g_out, "out", flat_b, B_ROWS)
    pack(g_gu, "gu", flat_b, B_ROWS)
    pack(g_down, "down", flat_b, B_ROWS)
    parts_b[...] = flat_b[...].reshape(parts_b.shape).astype(bf16)
    pack(g_in, "in", flat_a, A_ROWS)
    pack(g_qkv, "qkv", flat_a, A_ROWS)
    gain_rows(g_gain, flat_a)
    flat_a[pl.ds(5, 128, stride=A_ROWS), :] = jnp.broadcast_to(stats[...], (128, 128))
    parts_a[...] = flat_a[...].reshape(parts_a.shape)
    enter()
    a, b = Reduce(parts_a, half_a, row_a, line_a, sem_a), Reduce(parts_b, half_b, row_b, line_b, sem_b)
    for step in ("first", "second", "third"):
        getattr(a, step)()
        getattr(b, step)()
    tot_a = a.last()
    total_b[...] = b.last()
    finish(tot_a, total_b, running, o_in, o_qkv, o_out, o_gu, o_down, o_gain, o_running)


def finish(tot_a, total_b, running, o_in, o_qkv, o_out, o_gu, o_down, o_gain, o_running):
    for name, ref in (("in", o_in), ("qkv", o_qkv), ("out", o_out), ("gu", o_gu), ("down", o_down)):
        _, chunk, _, _, which, base = SPECS[name]
        for t, at, width in lane_tiles(chunk):
            ref[pl.ds(at, width)] = tot_a[base + t, :width] if which == "a" else total_b[base + t, :width]
    o_gain[0:1, :] = tot_a[0:1, 108:117]
    o_gain[1:2, :] = tot_a[0:1, 117:126]
    sums, counts = tot_a[5, :NSET], tot_a[5, NSET : 2 * NSET]
    old = running[...]
    o_running[...] = jnp.where(counts > 0.5, 0.75 * old + 0.25 * (sums / jnp.maximum(counts, 1.0)), old)


def reduce_all(grads, g_gain, stats, running):
    sd, V = jax.ShapeDtypeStruct, pltpu.VMEM
    return pl.pallas_call(
        reduce_kernel,
        in_specs=[VM] * 8,
        out_specs=[VM] * 7,
        out_shape=[sd((SPECS[n][1],), f32) for n in NAMES] + [sd((2, 9), f32), sd((NSET,), f32)],
        scratch_shapes=[V((128 * A_ROWS, 128), f32), V((128 * B_ROWS, 128), f32),
                        V((2, 16, 4, A_ROWS, 128), f32), V((2, 16, 4, B_ROWS, 128), bf16),
                        V((16, 4, A_ROWS, 128), f32), V((16, 4, B_ROWS, 128), bf16),
                        V((16, 4, A_ROWS, 128), f32), V((16, 4, B_ROWS, 128), bf16),
                        V((4, A_ROWS, 128), f32), V((4, B_ROWS, 128), bf16), V((B_ROWS, 128), f32)]
        + [pltpu.SemaphoreType.DMA((2, 3))] * 2,
        compiler_params=pltpu.CompilerParams(collective_id=1, has_side_effects=True, vmem_limit_bytes=40 * 2**20),
    )(*grads, g_gain, stats, running)


def fold(op, a):
    return op(a.reshape(a.shape[0] // 8, 8, a.shape[1]), axis=0)


def weave(gens):
    gens = list(gens)
    while gens:
        for g in list(gens):
            try:
                next(g)
            except StopIteration:
                gens.remove(g)


def attend(hh, count, q, k, v, prob, sbuf, rl, osum, mixed):
    diag = lambda c0: (lax.broadcasted_iota(jnp.int32, (CH, QT), 0) + c0) <= lax.broadcasted_iota(jnp.int32, (CH, QT), 1)
    kts = [k[hh * count + u].astype(f32).T.astype(bf16) for u in range(count)]
    tasks = [(u, j) for j in range(LEN // QT - 1, -1, -1) for u in range(count)]
    tops, invs = {}, {}

    def score(i):
        u, j = tasks[i]
        n, best = (j + 1) * QT, []
        for c in range(0, n, CH):
            s = dot(kts[u][c : c + CH], q[hh * count + u, :, j * QT : j * QT + QT])
            if c + CH > n - QT:
                s = jnp.where(diag(c - (n - QT)), s, -1e30)
            sbuf[i % 2, c : c + CH] = s
            best.append(fold(jnp.max, s))
            yield
        tops[i] = jnp.max(functools.reduce(jnp.maximum, best), axis=0, keepdims=True)

    def exponent(i):
        u, j = tasks[i]
        n, sums = (j + 1) * QT, []
        for c in range(0, n, CH):
            p = jnp.exp(sbuf[i % 2, c : c + CH] - tops[i])
            sums.append(fold(jnp.sum, p))
            prob[j][hh * count + u, c : c + CH] = p.astype(bf16)
            yield
        invs[i] = 1.0 / jnp.sum(functools.reduce(jnp.add, sums), axis=0, keepdims=True)

    def mix(i):
        u, j = tasks[i]
        h, n, cols = hh * count + u, (j + 1) * QT, pl.ds(j * QT, QT)
        o = dot(v[h][:, :n], prob[j][h]) * invs[i]
        rl[h, :, cols] = invs[i]
        osum[h, :, cols] = o
        mixed[h, :, cols] = o.astype(bf16)

    last = len(tasks)
    for i in range(last + 2):
        if 0 <= i - 2:
            mix(i - 2)
        weave(([score(i)] if i < last else []) + ([exponent(i - 1)] if 0 <= i - 1 < last else []))


def main_kernel(feats, dout, targets, lag_mask, date_mask, freq, sets, gains, cosr, sinr,
                win, wqkv, wout, wgu, wdown, winT, wqkvT, woutT, wguT, wdownT,
                out, gfeats, g_in, g_qkv, g_out, g_gu, g_down, g_gain, stats,
                factor, lifted, first, inv1, normed, q, k, v, p0, p1, p2, p3, sbuf, rl, osum, mixed, second, hidden, both,
                gmid, gbranch, gmixed, gjoint, gfirst):
    s = pl.program_id(0)
    prob = (p0, p1, p2, p3)

    @pl.when(s == 0)
    def _():
        for ref in (g_in, g_qkv, g_out, g_gu, g_down, g_gain):
            ref[...] = jnp.zeros_like(ref)
        series_scalars(targets, lag_mask, date_mask, freq, sets, factor, stats)

    def add_to(ref, val):
        for t, at, width in lane_tiles(val.shape[1]):
            ref[t, :, :width] += val[:, at : at + width]

    gain0 = gains[:, 0:1]
    gain1 = gains[:, 1:2]
    fac = jnp.where(s == 0, factor[:F, 0:1], factor[:F, 1:2])

    @pl.loop(0, LEN // TOK)
    def _(i):
        t = pl.ds(pl.multiple_of(i * TOK, TOK), TOK)
        lift = (feats[0, :, t].astype(f32) * fac).astype(bf16)
        lifted[:, t] = lift
        x = dot(winT[...], lift)
        first[:, t] = x
        r = lax.rsqrt(jnp.mean(x * x, axis=0, keepdims=True) + EPS)
        inv1[:, t] = r
        n = (x * r * gain0).astype(bf16)
        normed[:, t] = n
        joint = dot(wqkvT[...], n).reshape(3, H, HD, TOK)
        c, sn = cosr[:, t][None], sinr[:, t][None]
        for which, ref, scale in ((0, q, 0.25), (1, k, 1.0)):
            a, b = joint[which, :, :8], joint[which, :, 8:]
            ref[:, :, t] = (jnp.concatenate([a * c - b * sn, b * c + a * sn], axis=1) * scale).astype(bf16)
        v[:, :, t] = joint[2].astype(bf16)

    @pl.loop(0, H // 3)
    def _(hh):
        attend(hh, 3, q, k, v, prob, sbuf, rl, osum, mixed)

    @pl.loop(0, LEN // TOK)
    def _(i):
        t = pl.ds(pl.multiple_of(i * TOK, TOK), TOK)
        mid = first[:, t] + dot(woutT[...], mixed[:, :, t].reshape(D, TOK))
        r = lax.rsqrt(jnp.mean(mid * mid, axis=0, keepdims=True) + EPS)
        sec = (mid * r * gain1).astype(bf16)
        second[:, t] = sec
        g = dout[0, :, t]
        for f in range(0, FF, 128):
            gate = dot(wguT[f : f + 128], sec)
            up = dot(wguT[FF + f : FF + f + 128], sec)
            gh = dot(wdown[f : f + 128], g)
            sig = 1.0 / (1.0 + jnp.exp(-gate))
            silu = gate * sig
            hidden[f : f + 128, t] = (silu * up).astype(bf16)
            both[FF + f : FF + f + 128, t] = (gh * silu).astype(bf16)
            both[f : f + 128, t] = (gh * up * (sig + silu * (1.0 - sig))).astype(bf16)
        out[0, :, t] = (mid + dot(wdownT[...], hidden[:, t])).astype(bf16)
        c = dot(wgu[...], both[:, t])
        cg = c * gain1
        inner = jnp.mean(cg * mid, axis=0, keepdims=True)
        gain_part = c * mid * r
        g_gain[1] += gain_part[:, :128] + gain_part[:, 128:]
        gm = g.astype(f32) + r * cg - mid * (r * r * r * inner)
        gmid[:, t] = gm
        gb = gm.astype(bf16)
        gbranch[:, t] = gb
        gmixed[:, :, t] = dot(wout[...], gb).reshape(H, HD, TOK)

    add_to(g_down, dot(hidden[...], dout[0], 1, 1))
    add_to(g_gu, dot(second[...], both[...], 1, 1))
    add_to(g_out, dot(mixed[...].reshape(D, LEN), gbranch[...], 1, 1))

    @pl.loop(0, H)
    def _(h):
        do = (gmixed[h] * rl[h]).astype(bf16)
        delta = jnp.sum(do.astype(f32) * osum[h], axis=0, keepdims=True)
        vt = v[h].astype(f32).T.astype(bf16)
        kh = k[h]
        dk = jnp.zeros((HD, LEN), f32)
        dv = jnp.zeros((HD, LEN), f32)
        dqs = []
        for j in range(LEN // QT):
            n = (j + 1) * QT
            cols = slice(j * QT, n)
            dp = dot(vt[:n], do[:, cols])
            p = prob[j][h]
            ds = (p.astype(f32) * (dp - delta[:, cols])).astype(bf16)
            dqs.append(dot(kh[:, :n], ds))
            pad = lambda a: a if n == LEN else jnp.concatenate([a, jnp.zeros((HD, LEN - n), f32)], axis=1)
            dk += pad(dot(q[h, :, cols], ds, 1, 1))
            dv += pad(dot(do[:, cols], p, 1, 1))
        dq = jnp.concatenate(dqs, axis=1) * 0.25
        c, sn = cosr[...], sinr[...]
        for which, val in ((0, dq), (1, dk)):
            a, b = val[:8], val[8:]
            gjoint[which, h] = jnp.concatenate([a * c + b * sn, b * c - a * sn], axis=0).astype(bf16)
        gjoint[2, h] = dv.astype(bf16)

    @pl.loop(0, LEN // TOK)
    def _(i):
        t = pl.ds(pl.multiple_of(i * TOK, TOK), TOK)
        c = dot(wqkv[...], gjoint[:, :, :, t].reshape(3 * D, TOK))
        x, r = first[:, t], inv1[:, t]
        cg = c * gain0
        inner = jnp.mean(cg * x, axis=0, keepdims=True)
        gain_part = c * x * r
        g_gain[0] += gain_part[:, :128] + gain_part[:, 128:]
        gf = (gmid[:, t] + r * cg - x * (r * r * r * inner)).astype(bf16)
        gfirst[:, t] = gf
        gfeats[0, :, t] = (dot(win[...], gf) * fac).astype(bf16)

    add_to(g_qkv, dot(normed[...], gjoint[...].reshape(3 * D, LEN), 1, 1))
    add_to(g_in, dot(lifted[...], gfirst[...], 1, 1))


def run_main(feats_t, dout_t, targets, lag_mask, date_mask, freq_ids, dataset_ids, gain_cols, mats):
    cos, sin = rope_tables()
    S = feats_t.shape[0]
    full = lambda *shape: pl.BlockSpec(shape, lambda s: (0,) * len(shape))
    per = lambda *shape: pl.BlockSpec((1,) + shape, lambda s: (s,) + (0,) * len(shape))
    sd = jax.ShapeDtypeStruct
    V = pltpu.VMEM
    shapes = [(ROWS[n], SPECS[n][0]) for n in NAMES]
    return pl.pallas_call(
        main_kernel,
        grid=(S,),
        in_specs=[per(F, LEN), per(D, LEN), full(2, LEN), full(2, NLAG), full(2, NDATE), SM, SM, full(D, 2), full(8, LEN), full(8, LEN)]
        + [full(*s) for s in shapes]
        + [full(*s[::-1]) for s in shapes],
        out_specs=[per(D, LEN), per(F, LEN)] + [full(*tiled(n)) for n in NAMES] + [full(2, D, 128), full(1, 128)],
        out_shape=[sd((S, D, LEN), bf16), sd((S, F, LEN), bf16)] + [sd(tiled(n), f32) for n in NAMES] + [sd((2, D, 128), f32), sd((1, 128), f32)],
        scratch_shapes=[
            V((128, 8), f32),
            V((F, LEN), bf16), V((D, LEN), f32), V((1, LEN), f32), V((D, LEN), bf16),
            V((H, HD, LEN), bf16), V((H, HD, LEN), bf16), V((H, HD, LEN), bf16),
            *[V((H, (j + 1) * QT, QT), bf16) for j in range(4)],
            V((2, LEN, QT), f32), V((H, 1, LEN), f32), V((H, HD, LEN), f32), V((H, HD, LEN), bf16),
            V((D, LEN), bf16), V((FF, LEN), bf16), V((2 * FF, LEN), bf16),
            V((D, LEN), f32), V((D, LEN), bf16), V((H, HD, LEN), f32), V((3, H, HD, LEN), bf16), V((D, LEN), bf16),
        ],
        compiler_params=pltpu.CompilerParams(vmem_limit_bytes=60 * 2**20, dimension_semantics=("arbitrary",)),
    )(feats_t, dout_t, targets, lag_mask, date_mask, freq_ids, dataset_ids, gain_cols, jnp.asarray(cos), jnp.asarray(sin), *mats)


def body(feats, targets, lag_mask, date_mask, freq_ids, dataset_ids, w_in, w_qkv, w_out, w_gu, w_down, gains, running, d_out):
    *mats, gain_cols = gather_all(w_in, w_qkv, w_out, w_gu, w_down, gains)
    out, gfeats, *grads, g_gain, stats = run_main(
        jnp.swapaxes(feats, 1, 2), jnp.swapaxes(d_out, 1, 2), targets, lag_mask, date_mask, freq_ids, dataset_ids, gain_cols, mats
    )
    owned = reduce_all(grads, g_gain, stats, running)
    return (jnp.swapaxes(out, 1, 2), jnp.swapaxes(gfeats, 1, 2), *owned)


def solution(mesh):
    flat, rows, cube = P(BOTH), P(BOTH, None), P(BOTH, None, None)
    return jax.shard_map(
        body,
        mesh=mesh,
        in_specs=(cube, rows, rows, rows, flat, flat, flat, flat, flat, flat, flat, P(None, "dp"), P(), cube),
        out_specs=(cube, cube, flat, flat, flat, flat, flat, P(None, "dp"), P()),
        check_vma=False,
    )
```

time: 429 us -> 134 us (0.31)
  waiting for transfers between devices: 294 us -> 0 us
  Pallas kernels: 90.1 us -> 112 us
  between operations: 14.3 us -> 0.74 us
  local copies, waits for them, and re-layouts: 27.9 us -> 20.4 us
    unnamed x4 -> x0, waiting for transfers between devices: 294 us -> none
    pallas_call x0 -> x2, Pallas kernels: none -> 39 us  [the longest x1 21.7 us: gather_all(): pl.pallas_call(gather_kernel, in_specs=[VM] * 6, out_specs=[VM] * 11, out...]
    unnamed x22 -> x57, local copies, waits for them, and re-layouts: 1.25 us -> 20.4 us
    pallas_call x1, Pallas kernels: 90.1 us -> 73.1 us  [run_main(): pl.pallas_call(main_kernel, grid=(S,), in_specs=[per(F, LEN), per(D, LEN)...]
    reshape x14 -> x0, local copies, waits for them, and re-layouts: 9.73 us -> none  [the longest x5 4.38 us: body(): mats.append(gathered[:, at:at + size].reshape(shape))]
    slice x12 -> x0, local copies, waits for them, and re-layouts: 8.12 us -> none  [the longest x5 6.8 us: body(): outs.append(own[at:at + size])]
    concatenate x2 -> x0, local copies, waits for them, and re-layouts: 4.98 us -> none  [the longest x1 3.48 us: body(): jnp.concatenate([w_in, w_qkv, w_out, w_gu, w_down, gains.reshape(-1)])]
  transfers between devices with their start and end apart: 2 -> 0, of which waited for: 2 -> 0; matrix products, arithmetic and copies ran while one was open for 0% -> 0% of each run, Pallas kernels for 0% -> 0%
where the time goes in v2:
time: 134 us; the launch traced here: 133 us
  Pallas kernels  112 us (84%)
  local copies, waits for them, and re-layouts  20.4 us (15%)
    pallas_call x1, Pallas kernels, run_main(): pl.pallas_call(main_kernel, grid=(S,), in_specs=[per(F, LEN), per(D, LEN)...  73.1 us
    pallas_call x1, Pallas kernels, gather_all(): pl.pallas_call(gather_kernel, in_specs=[VM] * 6, out_specs=[VM] * 11, out...  21.7 us
    unnamed x57, local copies, waits for them, and re-layouts  20.4 us
    pallas_call x1, Pallas kernels, reduce_all(): pl.pallas_call(reduce_kernel, in_specs=[VM] * 8, out_specs=[VM] * 7, out_...  17.3 us

profile of v2, /device:TPU:1, one launch (start us, length us, event | category | flops | bytes accessed | tf_op | source)
XLA Modules:
  0.0 133.1 jit_solution(4440160086101464094)
XLA Ops:
  0.7 0.7 copy-done.18
  1.3 0.7 copy-done.17
  2.0 0.7 copy-done.23
  2.7 0.7 copy-done.24
  3.3 21.7 %shard_map.223 = (bf16[96,144]{1,0:T(8,128)(2,1)S(1)}, bf16[144,432]{1,0:T(8,128)(2,1)S(1)}, bf16[144,144]{1,0:T(8,128)(2,1)S(1)}, bf16[144,1024]{1,0:T(8,128)(2...) custom-call(bf16[108]{0:T(256)(128)(2,1)S(1)} %copy-done.22, ...), custom_call_target="tpu_custom_call" | custom-call | tf_op jit(solution)/shard_map/pallas_call | solution.py:307
  25.1 0.8 copy-done.2
  25.9 0.7 copy-done.3
  26.6 0.7 copy-done.5
  27.3 0.7 copy-done.6
  28.0 0.6 copy-done.9
  28.7 0.7 copy-done.10
  29.3 0.6 copy-done.12
  30.0 0.6 copy-done.13
  30.6 0.6 copy-done.14
  31.2 0.6 copy-done.15
  31.8 0.6 copy-done.16
  32.4 73.1 %shard_map.224 = (bf16[2,144,1024]{2,1,0:T(8,128)(2,1)}, bf16[2,96,1024]{2,1,0:T(8,128)(2,1)}, f32[2,96,128]{2,1,0:T(8,128)}, f32[4,144,128]{2,1,0:T(8,128)}, f3...) custom-call(bf16[2,96,1024]{2,1,0:T(8,128)(2,1)} %bitcast.5, ...), custom_call_target="tpu_custom_call" | custom-call | tf_op jit(solution)/shard_map/pallas_call | solution.py:559
  105.5 0.6 copy-done.20
  106.2 1.1 copy-done
  107.2 1.0 copy-done.1
  108.3 1.0 copy-done.4
  109.2 0.9 copy-done.7
  110.1 0.9 copy-done.8
  111.1 0.9 copy-done.11
  111.9 17.3 %shard_map.225 = (f32[108]{0:T(128)S(1)}, f32[486]{0:T(512)S(1)}, f32[162]{0:T(256)S(1)}, f32[1152]{0:T(1024)S(1)}, f32[576]{0:T(1024)S(1)}, /*index=5*/f32[2,9]{1,0:T(2,128)S(1)}, f32[8]{0:T(128)S(1)}) custom-call(f32[2,96,128]{2,1,0:T(8,128)S(1)} %copy-done.11, f32[4,144,128]{2,1,0:T(8,128)S(1)} %copy-done.4, f32[2,144,128]{2,1,0:T(8,128)S(1)} %copy-done.7, ...), custom_call_target="tpu_custom_call" | custom-call | tf_op jit(solution)/shard_map/pallas_call | solution.py:359
  129.2 0.5 copy.32
  129.7 0.6 copy.33
  130.3 0.6 copy.34
  130.9 0.6 copy.35
  131.5 0.6 copy.36
  132.1 0.6 copy.37
  132.6 0.5 copy.38
  (28 shorter events, 0.1 us)
Async XLA Ops:
  0.6 0.7 copy-start.18
  0.7 0.7 copy-start.19
  0.7 0.7 copy-start.22
  1.3 0.7 copy-start.17
  2.0 0.7 copy-start.23
  2.7 0.7 copy-start.24
  25.1 0.8 copy-start.2
  25.9 0.7 copy-start.3
  26.6 0.7 copy-start.5
  27.3 0.7 copy-start.6
  28.0 0.6 copy-start.9
  28.7 0.7 copy-start.10
  29.3 0.6 copy-start.12
  30.0 0.6 copy-start.13
  30.6 0.6 copy-start.14
  31.2 0.6 copy-start.15
  31.8 0.6 copy-start.16
  105.5 0.7 copy-start.20
  105.5 0.7 copy-start.21
  106.2 1.1 copy-start
  107.2 1.0 copy-start.1
  108.3 1.0 copy-start.4
  109.2 0.9 copy-start.7
  110.1 0.9 copy-start.8
  111.1 0.9 copy-start.11

commit v3 on v2

v3 whole, which is shorter than its diff:
```python
import functools

import jax
import jax.numpy as jnp
import numpy as np
from jax import lax
from jax.experimental import pallas as pl
from jax.experimental.pallas import tpu as pltpu
from jax.sharding import PartitionSpec as P

D, H, HD, FF, NDATE, NLAG, F, NSET, LEN = 144, 9, 16, 512, 12, 84, 96, 8, 1024
EPS = 1e-05
TOK = 256
QT = 256
CH = 128
f32, bf16 = jnp.float32, jnp.bfloat16
MESH = pl.DeviceIdType.MESH
BOTH = ("dp", "fsdp")

A_ROWS, B_ROWS = 8, 16
SPECS = {
    "in": (D, 108, 4, 3, "a", 0),
    "qkv": (3 * D, 486, 8, 9, "a", 1),
    "gu": (2 * FF, 1152, 8, 9, "b", 0),
    "down": (D, 576, 2, 8, "b", 9),
    "out": (D, 162, 8, 9, "b", 14),
}
ROWS = {"in": F, "qkv": D, "gu": D, "down": FF, "out": D}


def dot(a, b, ca=1, cb=0, **kw):
    return lax.dot_general(a, b, (((ca,), (cb,)), ((), ())), preferred_element_type=f32, **kw)


def lane_tiles(width):
    return [(t // 128, t, min(128, width - t)) for t in range(0, width, 128)]


def pieces(piece, source, count):
    cuts = []
    for i in range(count):
        at, left, parts = i * piece, piece, []
        while left:
            c, o = divmod(at, source)
            n = min(left, source - o)
            parts.append((c, o, n))
            at, left = at + n, left - n
        cuts.append(parts)
    return cuts


def spot(c):
    return (c % 2) * 64 + c // 2


def join(parts):
    return parts[0] if len(parts) == 1 else jnp.concatenate(parts, axis=1)


def unpack(flat, rows, name, dst):
    cols, chunk, gc, gr, _, base = SPECS[name]
    groups, kept = 128 // gc, {}

    def owner(c):
        if c not in kept:
            kept[c] = join(
                [flat[pl.ds(spot(c) * rows + base + t, groups, stride=gc // 2 * rows), :] for t, _, _ in lane_tiles(chunk)]
            )
        return kept[c]

    for i, parts in enumerate(pieces(cols, chunk, gr)):
        row = join([owner(c)[:, o : o + n] for c, o, n in parts])
        for t, at, width in lane_tiles(cols):
            dst[t, pl.ds(i, groups, stride=gr), :width] = row[:, at : at + width]


def pack(src, name, flat, rows):
    cols, chunk, gc, gr, _, base = SPECS[name]
    groups, kept = 128 // gc, {}

    def line(i):
        if i not in kept:
            kept[i] = join([src[t, pl.ds(i, groups, stride=gr), :] for t, _, _ in lane_tiles(cols)])
        return kept[i]

    for c, parts in enumerate(pieces(chunk, cols, gc)):
        run = [line(i)[:, o : o + n] for i, o, n in parts]
        run = join(run + ([jnp.zeros((groups, -chunk % 128), f32)] if chunk % 128 else []))
        for t, at, _ in lane_tiles(chunk):
            flat[pl.ds(spot(c) * rows + base + t, groups, stride=gc // 2 * rows), :] = run[:, at : at + 128]


def place():
    fs = lax.axis_index("fsdp")
    return lax.axis_index("dp"), fs // 2, fs % 2


def partners():
    dp, y, core = place()
    across = lambda o: (lax.rem(dp + o, 16), 2 * y + core)
    along = lambda o: (dp, 2 * lax.rem(y + o, 4) + core)
    return across, along, (dp, 2 * y + 1 - core)


def enter():
    across, along, sibling = partners()
    barrier = pltpu.get_barrier_semaphore()

    @pl.loop(1, 16)
    def _(o):
        pl.semaphore_signal(barrier, inc=1, device_id=across(o), device_id_type=MESH)

    for o in (1, 2, 3):
        pl.semaphore_signal(barrier, inc=1, device_id=along(o), device_id_type=MESH)
    pl.semaphore_signal(barrier, inc=1, device_id=sibling, device_id_type=MESH)
    pl.semaphore_wait(barrier, 19)


def send(src, dst, sems, k, to):
    pltpu.make_async_remote_copy(
        src_ref=src, dst_ref=dst, send_sem=sems.at[0, k], recv_sem=sems.at[1, k], device_id=to, device_id_type=MESH
    ).start()


def wait(ref, sem):
    pltpu.make_async_copy(ref, ref, sem).wait()


class Gather:
    def __init__(self, own, everyone, sems):
        self.own, self.all, self.sems = own, everyone, sems

    def first(self):
        dp, y, core = place()
        _, along, _ = partners()
        for o in (1, 2, 3):
            send(self.own, self.all.at[core, dp, y], self.sems, 0, along(o))
        self.all[core, dp, y] = self.own[...]

    def second(self):
        dp, y, core = place()
        across, _, _ = partners()
        wait(self.all.at[core, dp, pl.ds(0, 3)], self.sems.at[1, 0])
        wait(self.all.at[core, dp, pl.ds(0, 3)], self.sems.at[0, 0])
        line = self.all.at[core, dp]

        @pl.loop(1, 16)
        def _(o):
            send(line, line, self.sems, 1, across(o))

    def third(self):
        _, _, core = place()
        _, _, sibling = partners()
        wait(self.all.at[core, pl.ds(0, 15)], self.sems.at[1, 1])
        wait(self.all.at[core, pl.ds(0, 15)], self.sems.at[0, 1])
        send(self.all.at[core], self.all.at[core], self.sems, 2, sibling)

    def last(self):
        _, _, core = place()
        wait(self.all.at[core], self.sems.at[1, 2])
        wait(self.all.at[core], self.sems.at[0, 2])


class Reduce:
    def __init__(self, parts, half, row, line, sems):
        self.parts, self.half, self.row, self.line, self.sems = parts, half, row, line, sems

    def first(self):
        _, _, core = place()
        _, _, sibling = partners()
        send(self.parts.at[1 - core], self.half, self.sems, 0, sibling)

    def second(self):
        dp, y, core = place()
        across, _, _ = partners()
        wait(self.half, self.sems.at[1, 0])
        wait(self.half, self.sems.at[0, 0])
        self.half[...] = (self.half[...].astype(f32) + self.parts[core].astype(f32)).astype(self.half.dtype)

        @pl.loop(1, 16)
        def _(o):
            send(self.half.at[lax.rem(dp + o, 16)], self.row.at[dp], self.sems, 1, across(o))

        self.row[dp] = self.half[dp]

    def third(self):
        dp, y, core = place()
        _, along, _ = partners()
        wait(self.row.at[pl.ds(0, 15)], self.sems.at[1, 1])
        wait(self.row.at[pl.ds(0, 15)], self.sems.at[0, 1])
        mine = jnp.sum(self.row[...].astype(f32), axis=0).astype(self.row.dtype)
        self.half[0] = mine
        for o in (1, 2, 3):
            send(self.half.at[0, lax.rem(y + o, 4)], self.line.at[y], self.sems, 2, along(o))
        self.line[y] = self.half[0, y]

    def last(self):
        wait(self.line.at[pl.ds(0, 3)], self.sems.at[1, 2])
        wait(self.line.at[pl.ds(0, 3)], self.sems.at[0, 2])
        return jnp.sum(self.line[...].astype(f32), axis=0)


def rope_tables():
    freqs = np.float32(10000.0) ** (-np.arange(HD // 2, dtype=np.float32) * np.float32(2.0) / np.float32(HD))
    angle = np.arange(LEN, dtype=np.float32)[None, :] * freqs.astype(np.float32)[:, None]
    return np.cos(angle.astype(np.float64)).astype(np.float32), np.sin(angle.astype(np.float64)).astype(np.float32)


def own_tiles(w_in, w_qkv, w_out, w_gu, w_down, gains, tile_a, tile_b, wide):
    tile_a[...] = jnp.zeros_like(tile_a)
    wide[...] = jnp.zeros_like(wide)
    for name, ref in (("in", w_in), ("qkv", w_qkv), ("out", w_out), ("gu", w_gu), ("down", w_down)):
        _, chunk, _, _, which, base = SPECS[name]
        for t, at, width in lane_tiles(chunk):
            (tile_a if which == "a" else wide)[base + t, :width] = ref[pl.ds(at, width)].astype(f32)
    tile_a[0:1, 108:117] = gains[0:1, :].astype(f32)
    tile_a[0:1, 117:126] = gains[1:2, :].astype(f32)
    tile_b[...] = wide[...].astype(bf16)


def gain_columns(flat, out):
    rows = flat[pl.ds(0, 16, stride=4 * A_ROWS), :]
    r = lax.broadcasted_iota(jnp.int32, (D, 16), 0) // 9
    spread = dot((r == lax.broadcasted_iota(jnp.int32, (D, 16), 1)).astype(f32), rows)
    lane = lax.broadcasted_iota(jnp.int32, (D, 128), 1)
    e = lax.rem(lax.broadcasted_iota(jnp.int32, (D, 128), 0), 9)
    for i in (0, 1):
        out[:, i : i + 1] = jnp.sum(jnp.where(lane == e + 108 + 9 * i, spread, 0.0), axis=1, keepdims=True)


def gain_rows(partial, flat):
    pos = lax.broadcasted_iota(jnp.int32, (128, D), 0)
    r = lax.broadcasted_iota(jnp.int32, (128, D), 1) // 9
    pick = (lax.rem(pos, 64) // 4 == r).astype(f32)
    lane = lax.broadcasted_iota(jnp.int32, (D, 128), 1)
    e = lax.rem(lax.broadcasted_iota(jnp.int32, (D, 128), 0), 9)
    cols = jnp.zeros((D, 128), f32)
    for i in (0, 1):
        cols += jnp.where(lane == e + 108 + 9 * i, jnp.sum(partial[i], axis=1, keepdims=True), 0.0)
    spread = dot(pick, cols, precision=lax.Precision.HIGHEST)
    flat[pl.ds(0, 128, stride=A_ROWS), :] += spread


def series_scalars(targets, lag_mask, date_mask, freq, sets, factor, stats):
    scale = jnp.sum(jnp.abs(targets[...]), axis=1, keepdims=True) / LEN + 1e-5
    lag = lag_mask[...].astype(f32) / scale
    second = lax.broadcasted_iota(jnp.int32, (2, NDATE), 0) == 1
    start = jnp.where(second, freq[1], freq[0]) * (NDATE // 3)
    keep = jnp.where(lax.broadcasted_iota(jnp.int32, (2, NDATE), 1) >= start, date_mask[...], 0).astype(f32)
    both = jnp.concatenate([lag, keep], axis=1)
    both = jnp.concatenate([both, jnp.zeros((2, 32), f32)], axis=1)
    both = jnp.concatenate([both, jnp.zeros((6, 128), f32)], axis=0)
    factor[...] = both.T
    lane = lax.broadcasted_iota(jnp.int32, (1, 128), 1)
    row = jnp.zeros((1, 128), f32)
    for s in (0, 1):
        row += jnp.where(lane == sets[s], scale[s : s + 1], 0.0) + jnp.where(lane == sets[s] + NSET, 1.0, 0.0)
    stats[...] = row

def fold(op, a):
    return op(a.reshape(a.shape[0] // 8, 8, a.shape[1]), axis=0)


def weave(gens):
    gens = list(gens)
    while gens:
        for g in list(gens):
            try:
                next(g)
            except StopIteration:
                gens.remove(g)


VM = pl.BlockSpec(memory_space=pltpu.VMEM)
SM = pl.BlockSpec(memory_space=pltpu.SMEM)
HB = pl.BlockSpec(memory_space=pl.ANY)
NAMES = ("in", "qkv", "out", "gu", "down")


def tiled(name):
    return (-(-SPECS[name][0] // 128), ROWS[name], 128)


def attend(s, hh, count, q, k, v, prob, sbuf, rl, osum, mixed):
    diag = lambda c0: (lax.broadcasted_iota(jnp.int32, (CH, QT), 0) + c0) <= lax.broadcasted_iota(jnp.int32, (CH, QT), 1)
    kts = [k[s, hh * count + u].astype(f32).T.astype(bf16) for u in range(count)]
    tasks = [(u, j) for j in range(LEN // QT - 1, -1, -1) for u in range(count)]
    tops, invs = {}, {}

    def score(i):
        u, j = tasks[i]
        n, best = (j + 1) * QT, []
        for c in range(0, n, CH):
            x = dot(kts[u][c : c + CH], q[s, hh * count + u, :, j * QT : j * QT + QT])
            if c + CH > n - QT:
                x = jnp.where(diag(c - (n - QT)), x, -1e30)
            sbuf[i % 2, c : c + CH] = x
            best.append(fold(jnp.max, x))
            yield
        tops[i] = jnp.max(functools.reduce(jnp.maximum, best), axis=0, keepdims=True)

    def exponent(i):
        u, j = tasks[i]
        n, sums = (j + 1) * QT, []
        for c in range(0, n, CH):
            p = jnp.exp(sbuf[i % 2, c : c + CH] - tops[i])
            sums.append(fold(jnp.sum, p))
            prob[j][s, hh * count + u, c : c + CH] = p.astype(bf16)
            yield
        invs[i] = 1.0 / jnp.sum(functools.reduce(jnp.add, sums), axis=0, keepdims=True)

    def mix(i):
        u, j = tasks[i]
        h, n, cols = hh * count + u, (j + 1) * QT, pl.ds(j * QT, QT)
        o = dot(v[s, h][:, :n], prob[j][s, h]) * invs[i]
        rl[s, h, :, cols] = invs[i]
        osum[s, h, :, cols] = o
        mixed[s, h, :, cols] = o.astype(bf16)

    last = len(tasks)
    for i in range(last + 2):
        if 0 <= i - 2:
            mix(i - 2)
        weave(([score(i)] if i < last else []) + ([exponent(i - 1)] if 0 <= i - 1 < last else []))


def attend_back(s, h, q, k, v, prob, rl, osum, gmixed, cosr, sinr, gjoint):
    do = (gmixed[s, h] * rl[s, h]).astype(bf16)
    delta = jnp.sum(do.astype(f32) * osum[s, h], axis=0, keepdims=True)
    vt = v[s, h].astype(f32).T.astype(bf16)
    kh = k[s, h]
    dk = jnp.zeros((HD, LEN), f32)
    dv = jnp.zeros((HD, LEN), f32)
    dqs = []
    for j in range(LEN // QT):
        n = (j + 1) * QT
        cols = slice(j * QT, n)
        dp = dot(vt[:n], do[:, cols])
        p = prob[j][s, h]
        ds = (p.astype(f32) * (dp - delta[:, cols])).astype(bf16)
        dqs.append(dot(kh[:, :n], ds))
        pad = lambda a: a if n == LEN else jnp.concatenate([a, jnp.zeros((HD, LEN - n), f32)], axis=1)
        dk += pad(dot(q[s, h, :, cols], ds, 1, 1))
        dv += pad(dot(do[:, cols], p, 1, 1))
    dq = jnp.concatenate(dqs, axis=1) * 0.25
    c, sn = cosr[...], sinr[...]
    for which, val in ((0, dq), (1, dk)):
        a, b = val[:8], val[8:]
        gjoint[s, which, h] = jnp.concatenate([a * c + b * sn, b * c - a * sn], axis=0).astype(bf16)
    gjoint[s, 2, h] = dv.astype(bf16)


def layer_kernel(
    feats_h, targets_h, lag_h, date_h, freq, sets, w_in_h, w_qkv_h, w_out_h, w_gu_h, w_down_h, gains_h, dout_h, cos_h, sin_h,
    out_h, gfeats_h, tot_a, tot_b,
    feats, dout, targets, lag_mask, date_mask, w_in, w_qkv, w_out, w_gu, w_down, gains_own, cosr, sinr, out, gfeats,
    tile_a, tile_b, all_a, all_b, flat_a, flat_b, half_a, half_b, row_a, row_b, line_a, line_b,
    m_in, m_qkv, m_out, m_gu, m_down, win, wqkv, wout, wgu, wdown, winT, wqkvT, woutT, wguT, wdownT,
    gains, g_gain, factor, stats, lifted, first, inv1, normed, q, k, v, p0, p1, p2, p3, sbuf, rl, osum, mixed, second, hidden, both,
    gmid, gbranch, gmixed, gjoint, gfirst, sem_a, sem_b, sem_c, sem_d, sem_l,
):
    prob = (p0, p1, p2, p3)
    loads = [
        pltpu.make_async_copy(src, dst, sem_l.at[i])
        for i, (src, dst) in enumerate(
            (
                (w_in_h, w_in), (w_qkv_h, w_qkv), (w_out_h, w_out), (w_gu_h, w_gu), (w_down_h, w_down), (gains_h, gains_own),
                (feats_h, feats), (targets_h, targets), (lag_h, lag_mask), (date_h, date_mask), (cos_h, cosr), (sin_h, sinr), (dout_h, dout),
            )
        )
    ]
    for load in loads:
        load.start()
    for load in loads[:6]:
        load.wait()
    own_tiles(w_in, w_qkv, w_out, w_gu, w_down, gains_own, tile_a, tile_b, flat_b.at[pl.ds(0, B_ROWS)])
    enter()
    a, b = Gather(tile_a, all_a, sem_a), Gather(tile_b, all_b, sem_b)
    a.first()
    b.first()
    for load in loads[6:12]:
        load.wait()
    series_scalars(targets, lag_mask, date_mask, freq, sets, factor, stats)
    g_gain[...] = jnp.zeros_like(g_gain)
    for s in (0, 1):
        lifted[s] = (feats[s].astype(f32) * factor[:F, s : s + 1]).astype(bf16)
    a.second()
    a.third()
    b.second()
    a.last()
    flat_a[...] = all_a[...].reshape(128 * A_ROWS, 128)
    gain_columns(flat_a, gains)

    def emit(name, flat, rows, mat, out, outT):
        unpack(flat, rows, name, mat)
        for t, at, width in lane_tiles(SPECS[name][0]):
            val = mat[t][:, :width]
            out[:, at : at + width] = val.astype(bf16)
            outT[at : at + width, :] = val.T.astype(bf16)
        mat[...] = jnp.zeros_like(mat)

    emit("in", flat_a, A_ROWS, m_in, win, winT)
    emit("qkv", flat_a, A_ROWS, m_qkv, wqkv, wqkvT)

    def add_to(ref, val):
        for t, at, width in lane_tiles(val.shape[1]):
            ref[t, :, :width] += val[:, at : at + width]

    gain0 = gains[:, 0:1]
    gain1 = gains[:, 1:2]

    @pl.loop(0, 2)
    def _(s):
        @pl.loop(0, LEN // TOK)
        def _(i):
            t = pl.ds(pl.multiple_of(i * TOK, TOK), TOK)
            x = dot(winT[...], lifted[s, :, t])
            first[s, :, t] = x
            r = lax.rsqrt(jnp.mean(x * x, axis=0, keepdims=True) + EPS)
            inv1[s, :, t] = r
            n = (x * r * gain0).astype(bf16)
            normed[s, :, t] = n
            joint = dot(wqkvT[...], n).reshape(3, H, HD, TOK)
            c, sn = cosr[:, t][None], sinr[:, t][None]
            for which, ref, scale in ((0, q, 0.25), (1, k, 1.0)):
                u, w = joint[which, :, :8], joint[which, :, 8:]
                ref[s, :, :, t] = (jnp.concatenate([u * c - w * sn, w * c + u * sn], axis=1) * scale).astype(bf16)
            v[s, :, :, t] = joint[2].astype(bf16)

    @pl.loop(0, H // 3)
    def _(hh):
        attend(0, hh, 3, q, k, v, prob, sbuf, rl, osum, mixed)

    b.third()

    @pl.loop(0, H // 3)
    def _(hh):
        attend(1, hh, 3, q, k, v, prob, sbuf, rl, osum, mixed)

    b.last()
    flat_b[...] = all_b[...].astype(f32).reshape(128 * B_ROWS, 128)
    emit("out", flat_b, B_ROWS, m_out, wout, woutT)
    emit("gu", flat_b, B_ROWS, m_gu, wgu, wguT)
    emit("down", flat_b, B_ROWS, m_down, wdown, wdownT)
    loads[12].wait()

    @pl.loop(0, 2)
    def _(s):
        @pl.loop(0, LEN // TOK)
        def _(i):
            t = pl.ds(pl.multiple_of(i * TOK, TOK), TOK)
            mid = first[s, :, t] + dot(woutT[...], mixed[s, :, :, t].reshape(D, TOK))
            r = lax.rsqrt(jnp.mean(mid * mid, axis=0, keepdims=True) + EPS)
            sec = (mid * r * gain1).astype(bf16)
            second[:, t] = sec
            g = dout[s, :, t]
            for f in range(0, FF, 128):
                gate = dot(wguT[f : f + 128], sec)
                up = dot(wguT[FF + f : FF + f + 128], sec)
                gh = dot(wdown[f : f + 128], g)
                sig = 1.0 / (1.0 + jnp.exp(-gate))
                silu = gate * sig
                hidden[f : f + 128, t] = (silu * up).astype(bf16)
                both[FF + f : FF + f + 128, t] = (gh * silu).astype(bf16)
                both[f : f + 128, t] = (gh * up * (sig + silu * (1.0 - sig))).astype(bf16)
            out[s, :, t] = (mid + dot(wdownT[...], hidden[:, t])).astype(bf16)
            c = dot(wgu[...], both[:, t])
            cg = c * gain1
            inner = jnp.mean(cg * mid, axis=0, keepdims=True)
            gain_part = c * mid * r
            g_gain[1] += gain_part[:, :128] + gain_part[:, 128:]
            gm = g.astype(f32) + r * cg - mid * (r * r * r * inner)
            gmid[s, :, t] = gm
            gb = gm.astype(bf16)
            gbranch[:, t] = gb
            gmixed[s, :, :, t] = dot(wout[...], gb).reshape(H, HD, TOK)

        add_to(m_down, dot(hidden[...], dout[s], 1, 1))
        add_to(m_gu, dot(second[...], both[...], 1, 1))
        add_to(m_out, dot(mixed[s].reshape(D, LEN), gbranch[...], 1, 1))

    store_out = pltpu.make_async_copy(out, out_h, sem_l.at[13])
    store_out.start()
    flat_b[...] = jnp.zeros_like(flat_b)
    pack(m_out, "out", flat_b, B_ROWS)
    pack(m_gu, "gu", flat_b, B_ROWS)
    pack(m_down, "down", flat_b, B_ROWS)
    all_b[...] = flat_b[...].reshape(all_b.shape).astype(bf16)
    a, b = Reduce(all_a, half_a, row_a, line_a, sem_c), Reduce(all_b, half_b, row_b, line_b, sem_d)
    b.first()

    @pl.loop(0, H)
    def _(h):
        attend_back(0, h, q, k, v, prob, rl, osum, gmixed, cosr, sinr, gjoint)

    b.second()

    @pl.loop(0, H)
    def _(h):
        attend_back(1, h, q, k, v, prob, rl, osum, gmixed, cosr, sinr, gjoint)

    b.third()

    @pl.loop(0, 2)
    def _(s):
        add_to(m_qkv, dot(normed[s], gjoint[s].reshape(3 * D, LEN), 1, 1))
        fac = jnp.where(s == 0, factor[:F, 0:1], factor[:F, 1:2])

        @pl.loop(0, LEN // TOK)
        def _(i):
            t = pl.ds(pl.multiple_of(i * TOK, TOK), TOK)
            c = dot(wqkv[...], gjoint[s, :, :, :, t].reshape(3 * D, TOK))
            x, r = first[s, :, t], inv1[s, :, t]
            cg = c * gain0
            inner = jnp.mean(cg * x, axis=0, keepdims=True)
            gain_part = c * x * r
            g_gain[0] += gain_part[:, :128] + gain_part[:, 128:]
            gf = (gmid[s, :, t] + r * cg - x * (r * r * r * inner)).astype(bf16)
            gfirst[:, t] = gf
            gfeats[s, :, t] = (dot(win[...], gf) * fac).astype(bf16)

        add_to(m_in, dot(lifted[s], gfirst[...], 1, 1))

    store_gfeats = pltpu.make_async_copy(gfeats, gfeats_h, sem_l.at[14])
    store_gfeats.start()
    flat_a[...] = jnp.zeros_like(flat_a)
    pack(m_in, "in", flat_a, A_ROWS)
    pack(m_qkv, "qkv", flat_a, A_ROWS)
    gain_rows(g_gain, flat_a)
    flat_a[pl.ds(5, 128, stride=A_ROWS), :] = jnp.broadcast_to(stats[...], (128, 128))
    all_a[...] = flat_a[...].reshape(all_a.shape)
    a.first()
    a.second()
    tot_b[...] = b.last()
    a.third()
    tot_a[...] = a.last()
    store_out.wait()
    store_gfeats.wait()


def run_layer(feats_t, targets, lag_mask, date_mask, freq_ids, dataset_ids, weights, gains, dout_t):
    cos, sin = rope_tables()
    sd, V = jax.ShapeDtypeStruct, pltpu.VMEM
    shapes = [(ROWS[n], SPECS[n][0]) for n in NAMES]
    return pl.pallas_call(
        layer_kernel,
        in_specs=[HB] * 4 + [SM] * 2 + [HB] * 9,
        out_specs=[HB, HB, VM, VM],
        out_shape=[sd((2, D, LEN), bf16), sd((2, F, LEN), bf16), sd((A_ROWS, 128), f32), sd((B_ROWS, 128), f32)],
        scratch_shapes=[
            V((2, F, LEN), bf16), V((2, D, LEN), bf16), V((2, LEN), f32), V((2, NLAG), jnp.int32), V((2, NDATE), jnp.int32),
            *[V((SPECS[n][1],), bf16) for n in NAMES], V((2, 9), bf16), V((8, LEN), f32), V((8, LEN), f32),
            V((2, D, LEN), bf16), V((2, F, LEN), bf16),
            V((A_ROWS, 128), f32), V((B_ROWS, 128), bf16),
            V((2, 16, 4, A_ROWS, 128), f32), V((2, 16, 4, B_ROWS, 128), bf16),
            V((128 * A_ROWS, 128), f32), V((128 * B_ROWS, 128), f32),
            V((16, 4, A_ROWS, 128), f32), V((16, 4, B_ROWS, 128), bf16),
            V((16, 4, A_ROWS, 128), f32), V((16, 4, B_ROWS, 128), bf16),
            V((4, A_ROWS, 128), f32), V((4, B_ROWS, 128), bf16),
            *[V(tiled(n), f32) for n in NAMES], *[V(s, bf16) for s in shapes], *[V(s[::-1], bf16) for s in shapes],
            V((D, 2), f32), V((2, D, 128), f32), V((128, 8), f32), V((1, 128), f32),
            V((2, F, LEN), bf16), V((2, D, LEN), f32), V((2, 1, LEN), f32), V((2, D, LEN), bf16),
            V((2, H, HD, LEN), bf16), V((2, H, HD, LEN), bf16), V((2, H, HD, LEN), bf16),
            *[V((2, H, (j + 1) * QT, QT), bf16) for j in range(4)],
            V((2, LEN, QT), f32), V((2, H, 1, LEN), f32), V((2, H, HD, LEN), f32), V((2, H, HD, LEN), bf16),
            V((D, LEN), bf16), V((FF, LEN), bf16), V((2 * FF, LEN), bf16),
            V((2, D, LEN), f32), V((D, LEN), bf16), V((2, H, HD, LEN), f32), V((2, 3, H, HD, LEN), bf16), V((D, LEN), bf16),
            *[pltpu.SemaphoreType.DMA((2, 3))] * 4, pltpu.SemaphoreType.DMA((15,)),
        ],
        compiler_params=pltpu.CompilerParams(collective_id=0, has_side_effects=True, vmem_limit_bytes=63 * 2**20),
    )(feats_t, targets, lag_mask, date_mask, freq_ids, dataset_ids, *weights, gains, dout_t, jnp.asarray(cos), jnp.asarray(sin))


def finish_kernel(out_h, gfeats_h, tot_a_h, tot_b_h, running_h, out, gfeats, o_in, o_qkv, o_out, o_gu, o_down, o_gain, o_running,
                  tot_a, tot_b, running, sems):
    pairs = ((out_h, out), (gfeats_h, gfeats), (tot_a_h, tot_a), (tot_b_h, tot_b), (running_h, running))
    copies = [pltpu.make_async_copy(src, dst, sems.at[i]) for i, (src, dst) in enumerate(pairs)]
    for copy in copies:
        copy.start()
    for copy in copies[2:]:
        copy.wait()
    for name, ref in (("in", o_in), ("qkv", o_qkv), ("out", o_out), ("gu", o_gu), ("down", o_down)):
        _, chunk, _, _, which, base = SPECS[name]
        for t, at, width in lane_tiles(chunk):
            ref[pl.ds(at, width)] = (tot_a if which == "a" else tot_b)[base + t, :width]
    o_gain[0:1, :] = tot_a[0:1, 108:117]
    o_gain[1:2, :] = tot_a[0:1, 117:126]
    sums, counts = tot_a[5, :NSET], tot_a[5, NSET : 2 * NSET]
    old = running[...]
    o_running[...] = jnp.where(counts > 0.5, 0.75 * old + 0.25 * (sums / jnp.maximum(counts, 1.0)), old)
    for copy in copies[:2]:
        copy.wait()


def hand_out(out, gfeats, tot_a, tot_b, running):
    sd, V = jax.ShapeDtypeStruct, pltpu.VMEM
    return pl.pallas_call(
        finish_kernel,
        in_specs=[HB] * 5,
        out_specs=[HB, HB] + [VM] * 7,
        out_shape=[sd((2, D, LEN), bf16), sd((2, F, LEN), bf16)]
        + [sd((SPECS[n][1],), f32) for n in NAMES] + [sd((2, 9), f32), sd((NSET,), f32)],
        scratch_shapes=[V((A_ROWS, 128), f32), V((B_ROWS, 128), f32), V((NSET,), f32), pltpu.SemaphoreType.DMA((5,))],
        compiler_params=pltpu.CompilerParams(vmem_limit_bytes=60 * 2**20),
    )(out, gfeats, tot_a, tot_b, running)


def body(feats, targets, lag_mask, date_mask, freq_ids, dataset_ids, w_in, w_qkv, w_out, w_gu, w_down, gains, running, d_out):
    done = run_layer(
        jnp.swapaxes(feats, 1, 2), targets, lag_mask, date_mask, freq_ids, dataset_ids,
        (w_in, w_qkv, w_out, w_gu, w_down), gains, jnp.swapaxes(d_out, 1, 2),
    )
    out, gfeats, *rest = hand_out(*done, running)
    return (jnp.swapaxes(out, 1, 2), jnp.swapaxes(gfeats, 1, 2), *rest)


def solution(mesh):
    flat, rows, cube = P(BOTH), P(BOTH, None), P(BOTH, None, None)
    return jax.shard_map(
        body,
        mesh=mesh,
        in_specs=(cube, rows, rows, rows, flat, flat, flat, flat, flat, flat, flat, P(None, "dp"), P(), cube),
        out_specs=(cube, cube, flat, flat, flat, flat, flat, P(None, "dp"), P()),
        check_vma=False,
    )
```

time: 134 us -> 136 us (1.015)
  Pallas kernels: 112 us -> 134 us
  local copies, waits for them, and re-layouts: 20.4 us -> 0 us
    pallas_call x3 -> x2, Pallas kernels: 112 us -> 134 us  [the longest x1 102 us: run_layer(): pl.pallas_call(layer_kernel, in_specs=[HB] * 4 + [SM] * 2 + [HB] * 9, out...]
    unnamed x57 -> x0, local copies, waits for them, and re-layouts: 20.4 us -> none
where the time goes in v3:
time: 136 us; the launch traced here: 134 us
  Pallas kernels  134 us (99%)
    pallas_call x1, Pallas kernels, run_layer(): pl.pallas_call(layer_kernel, in_specs=[HB] * 4 + [SM] * 2 + [HB] * 9, out...  102 us
    pallas_call x1, Pallas kernels, hand_out(): pl.pallas_call(finish_kernel, in_specs=[HB] * 5, out_specs=[HB, HB] + [VM...  31.5 us

profile of v3, /device:TPU:1, one launch (start us, length us, event | category | flops | bytes accessed | tf_op | source)
XLA Modules:
  0.0 134.4 jit_solution(11745873299538057140)
XLA Ops:
  0.6 102.2 %shard_map.223 = (bf16[2,144,1024]{2,1,0:T(8,128)(2,1)}, bf16[2,96,1024]{2,1,0:T(8,128)(2,1)}, f32[8,128]{1,0:T(8,128)}, f32[16,128]{1,0:T(8,128)}) custom-call(bf16[2,96,1024]{2,1,0:T(8,128)(2,1)} %bitcast.5, f32[2,1024]{1,0:T(2,128)} %targets_h.1, s32[2,84]{1,0:T(2,128)} %lag_h.1, s32[2,12]{1,0:T(2,128)} %date_h.1, s32[2]{0:T(128)} %freq.1, s32[2]{0:T(128)} %sets.1, ...), custom_call_target="tpu_custom_call" | custom-call | tf_op jit(solution)/shard_map/pallas_call | solution.py:545
  102.8 31.5 %shard_map.224 = (bf16[2,144,1024]{2,1,0:T(8,128)(2,1)}, bf16[2,96,1024]{2,1,0:T(8,128)(2,1)}, f32[108]{0:T(128)}, f32[486]{0:T(512)}, f32[162]{0:T(256)}, /*ind...) custom-call(bf16[2,144,1024]{2,1,0:T(8,128)(2,1)} %get-tuple-element.22.out_h, ...), custom_call_target="tpu_custom_call" | custom-call | tf_op jit(solution)/shard_map/pallas_call | solution.py:597

commit v4 on v3

--- a/solution.py
+++ b/solution.py
@@ -13,6 +13,7 @@
 TOK = 256
 QT = 256
 CH = 128
+GROUP = 3
 f32, bf16 = jnp.float32, jnp.bfloat16
 MESH = pl.DeviceIdType.MESH
 BOTH = ("dp", "fsdp")
@@ -281,73 +282,99 @@
     return (-(-SPECS[name][0] // 128), ROWS[name], 128)
 
 
-def attend(s, hh, count, q, k, v, prob, sbuf, rl, osum, mixed):
+def attend(s, hh, q, k, v, prob, sbuf, rl, osum, mixed):
     diag = lambda c0: (lax.broadcasted_iota(jnp.int32, (CH, QT), 0) + c0) <= lax.broadcasted_iota(jnp.int32, (CH, QT), 1)
-    kts = [k[s, hh * count + u].astype(f32).T.astype(bf16) for u in range(count)]
-    tasks = [(u, j) for j in range(LEN // QT - 1, -1, -1) for u in range(count)]
-    tops, invs = {}, {}
+    heads = [hh * GROUP + u for u in range(GROUP)]
+    kts = [k[s, h].astype(f32).T.astype(bf16) for h in heads]
+    ones = (lax.broadcasted_iota(jnp.int32, (HD, LEN), 0) == 0).astype(f32).astype(bf16)
+    vs = [jnp.concatenate([v[s, h], ones], axis=0) for h in heads]
+    tasks = [(u, j) for j in range(LEN // QT - 1, -1, -1) for u in range(GROUP)]
+    tops = {}
 
     def score(i):
         u, j = tasks[i]
-        n, best = (j + 1) * QT, []
+        n, best = (j + 1) * QT, None
         for c in range(0, n, CH):
-            x = dot(kts[u][c : c + CH], q[s, hh * count + u, :, j * QT : j * QT + QT])
+            x = dot(kts[u][c : c + CH], q[s, heads[u], :, j * QT : j * QT + QT])
             if c + CH > n - QT:
                 x = jnp.where(diag(c - (n - QT)), x, -1e30)
             sbuf[i % 2, c : c + CH] = x
-            best.append(fold(jnp.max, x))
+            top = fold(jnp.max, x)
+            best = top if best is None else jnp.maximum(best, top)
             yield
-        tops[i] = jnp.max(functools.reduce(jnp.maximum, best), axis=0, keepdims=True)
+        tops[i] = jnp.max(best, axis=0, keepdims=True)
 
     def exponent(i):
         u, j = tasks[i]
-        n, sums = (j + 1) * QT, []
-        for c in range(0, n, CH):
-            p = jnp.exp(sbuf[i % 2, c : c + CH] - tops[i])
-            sums.append(fold(jnp.sum, p))
-            prob[j][s, hh * count + u, c : c + CH] = p.astype(bf16)
+        for c in range(0, (j + 1) * QT, CH):
+            prob[j][s, heads[u], c : c + CH] = jnp.exp(sbuf[i % 2, c : c + CH] - tops[i]).astype(bf16)
             yield
-        invs[i] = 1.0 / jnp.sum(functools.reduce(jnp.add, sums), axis=0, keepdims=True)
 
     def mix(i):
         u, j = tasks[i]
-        h, n, cols = hh * count + u, (j + 1) * QT, pl.ds(j * QT, QT)
-        o = dot(v[s, h][:, :n], prob[j][s, h]) * invs[i]
-        rl[s, h, :, cols] = invs[i]
+        h, n, cols = heads[u], (j + 1) * QT, pl.ds(j * QT, QT)
+        o = dot(vs[u][:, :n], prob[j][s, h])
+        inv = 1.0 / o[HD : HD + 1]
+        o = o[:HD] * inv
+        rl[s, h, :, cols] = inv
         osum[s, h, :, cols] = o
         mixed[s, h, :, cols] = o.astype(bf16)
 
     last = len(tasks)
-    for i in range(last + 2):
-        if 0 <= i - 2:
-            mix(i - 2)
+    for i in range(last + 3):
+        if 0 <= i - 3:
+            mix(i - 3)
         weave(([score(i)] if i < last else []) + ([exponent(i - 1)] if 0 <= i - 1 < last else []))
 
 
-def attend_back(s, h, q, k, v, prob, rl, osum, gmixed, cosr, sinr, gjoint):
-    do = (gmixed[s, h] * rl[s, h]).astype(bf16)
-    delta = jnp.sum(do.astype(f32) * osum[s, h], axis=0, keepdims=True)
-    vt = v[s, h].astype(f32).T.astype(bf16)
-    kh = k[s, h]
-    dk = jnp.zeros((HD, LEN), f32)
-    dv = jnp.zeros((HD, LEN), f32)
-    dqs = []
-    for j in range(LEN // QT):
+def attend_back(s, hh, q, k, v, prob, rl, osum, gmixed, cosr, sinr, gjoint, dsb, dq, dk, dv):
+    heads = [hh * GROUP + u for u in range(GROUP)]
+    dos, deltas, vts = [], [], []
+    for h in heads:
+        do = (gmixed[s, h] * rl[s, h]).astype(bf16)
+        dos.append(do)
+        deltas.append(jnp.sum(do.astype(f32) * osum[s, h], axis=0, keepdims=True))
+        vts.append(v[s, h].astype(f32).T.astype(bf16))
+    dk[...] = jnp.zeros_like(dk)
+    dv[...] = jnp.zeros_like(dv)
+    tasks = [(u, j) for j in range(LEN // QT - 1, -1, -1) for u in range(GROUP)]
+
+    def spread(i):
+        u, j = tasks[i]
         n = (j + 1) * QT
         cols = slice(j * QT, n)
-        dp = dot(vt[:n], do[:, cols])
-        p = prob[j][s, h]
-        ds = (p.astype(f32) * (dp - delta[:, cols])).astype(bf16)
-        dqs.append(dot(kh[:, :n], ds))
-        pad = lambda a: a if n == LEN else jnp.concatenate([a, jnp.zeros((HD, LEN - n), f32)], axis=1)
-        dk += pad(dot(q[s, h, :, cols], ds, 1, 1))
-        dv += pad(dot(do[:, cols], p, 1, 1))
-    dq = jnp.concatenate(dqs, axis=1) * 0.25
+        for c in range(0, n, QT):
+            dp = dot(vts[u][c : c + QT], dos[u][:, cols]) - deltas[u][:, cols]
+            dsb[i % 2, c : c + QT] = (prob[j][s, heads[u], c : c + QT].astype(f32) * dp).astype(bf16)
+            yield
+
+    def to_query(i):
+        u, j = tasks[i]
+        n = (j + 1) * QT
+        dq[u, :, j * QT : n] = dot(k[s, heads[u]][:, :n], dsb[i % 2, :n])
+        yield
+
+    def to_keys(i):
+        u, j = tasks[i]
+        for c in range(0, (j + 1) * QT, QT):
+            dk[u, :, c : c + QT] += dot(q[s, heads[u], :, j * QT : j * QT + QT], dsb[i % 2, c : c + QT], 1, 1)
+            yield
+
+    def to_values(i):
+        u, j = tasks[i]
+        for c in range(0, (j + 1) * QT, QT):
+            dv[u, :, c : c + QT] += dot(dos[u][:, j * QT : j * QT + QT], prob[j][s, heads[u], c : c + QT], 1, 1)
+            yield
+
+    last = len(tasks)
+    for i in range(last + 1):
+        weave(([spread(i)] if i < last else []) + ([to_query(i - 1), to_keys(i - 1), to_values(i - 1)] if i else []))
     c, sn = cosr[...], sinr[...]
-    for which, val in ((0, dq), (1, dk)):
-        a, b = val[:8], val[8:]
-        gjoint[s, which, h] = jnp.concatenate([a * c + b * sn, b * c - a * sn], axis=0).astype(bf16)
-    gjoint[s, 2, h] = dv.astype(bf16)
+    for u, h in enumerate(heads):
+        for which, val in ((0, dq[u] * 0.25), (1, dk[u])):
+            a, b = val[:8], val[8:]
+            gjoint[s, which, h] = jnp.concatenate([a * c + b * sn, b * c - a * sn], axis=0).astype(bf16)
+        gjoint[s, 2, h] = dv[u].astype(bf16)
 
 
 def layer_kernel(
@@ -357,7 +384,7 @@
     tile_a, tile_b, all_a, all_b, flat_a, flat_b, half_a, half_b, row_a, row_b, line_a, line_b,
     m_in, m_qkv, m_out, m_gu, m_down, win, wqkv, wout, wgu, wdown, winT, wqkvT, woutT, wguT, wdownT,
     gains, g_gain, factor, stats, lifted, first, inv1, normed, q, k, v, p0, p1, p2, p3, sbuf, rl, osum, mixed, second, hidden, both,
-    gmid, gbranch, gmixed, gjoint, gfirst, sem_a, sem_b, sem_c, sem_d, sem_l,
+    gmid, gbranch, gmixed, gjoint, gfirst, dsb, dq, dk, dv, sem_a, sem_b, sem_c, sem_d, sem_l,
 ):
     prob = (p0, p1, p2, p3)
     loads = [
@@ -427,15 +454,15 @@
                 ref[s, :, :, t] = (jnp.concatenate([u * c - w * sn, w * c + u * sn], axis=1) * scale).astype(bf16)
             v[s, :, :, t] = joint[2].astype(bf16)
 
-    @pl.loop(0, H // 3)
+    @pl.loop(0, H // GROUP)
     def _(hh):
-        attend(0, hh, 3, q, k, v, prob, sbuf, rl, osum, mixed)
+        attend(0, hh, q, k, v, prob, sbuf, rl, osum, mixed)
 
     b.third()
 
-    @pl.loop(0, H // 3)
+    @pl.loop(0, H // GROUP)
     def _(hh):
-        attend(1, hh, 3, q, k, v, prob, sbuf, rl, osum, mixed)
+        attend(1, hh, q, k, v, prob, sbuf, rl, osum, mixed)
 
     b.last()
     flat_b[...] = all_b[...].astype(f32).reshape(128 * B_ROWS, 128)
@@ -489,15 +516,15 @@
     a, b = Reduce(all_a, half_a, row_a, line_a, sem_c), Reduce(all_b, half_b, row_b, line_b, sem_d)
     b.first()
 
-    @pl.loop(0, H)
-    def _(h):
-        attend_back(0, h, q, k, v, prob, rl, osum, gmixed, cosr, sinr, gjoint)
+    @pl.loop(0, H // GROUP)
+    def _(hh):
+        attend_back(0, hh, q, k, v, prob, rl, osum, gmixed, cosr, sinr, gjoint, dsb, dq, dk, dv)
 
     b.second()
 
-    @pl.loop(0, H)
-    def _(h):
-        attend_back(1, h, q, k, v, prob, rl, osum, gmixed, cosr, sinr, gjoint)
+    @pl.loop(0, H // GROUP)
+    def _(hh):
+        attend_back(1, hh, q, k, v, prob, rl, osum, gmixed, cosr, sinr, gjoint, dsb, dq, dk, dv)
 
     b.third()
 
@@ -565,6 +592,7 @@
             V((2, LEN, QT), f32), V((2, H, 1, LEN), f32), V((2, H, HD, LEN), f32), V((2, H, HD, LEN), bf16),
             V((D, LEN), bf16), V((FF, LEN), bf16), V((2 * FF, LEN), bf16),
             V((2, D, LEN), f32), V((D, LEN), bf16), V((2, H, HD, LEN), f32), V((2, 3, H, HD, LEN), bf16), V((D, LEN), bf16),
+            V((2, LEN, QT), bf16), *[V((GROUP, HD, LEN), f32)] * 3,
             *[pltpu.SemaphoreType.DMA((2, 3))] * 4, pltpu.SemaphoreType.DMA((15,)),
         ],
         compiler_params=pltpu.CompilerParams(collective_id=0, has_side_effects=True, vmem_limit_bytes=63 * 2**20),
@@ -572,13 +600,16 @@
 
 
 def finish_kernel(out_h, gfeats_h, tot_a_h, tot_b_h, running_h, out, gfeats, o_in, o_qkv, o_out, o_gu, o_down, o_gain, o_running,
-                  tot_a, tot_b, running, sems):
-    pairs = ((out_h, out), (gfeats_h, gfeats), (tot_a_h, tot_a), (tot_b_h, tot_b), (running_h, running))
+                  out_v, gfeats_v, tot_a, tot_b, running, sems):
+    pairs = ((tot_a_h, tot_a), (tot_b_h, tot_b), (running_h, running), (out_h, out_v), (gfeats_h, gfeats_v))
     copies = [pltpu.make_async_copy(src, dst, sems.at[i]) for i, (src, dst) in enumerate(pairs)]
+    stores = [pltpu.make_async_copy(src, dst, sems.at[5 + i]) for i, (src, dst) in enumerate(((out_v, out), (gfeats_v, gfeats)))]
     for copy in copies:
         copy.start()
-    for copy in copies[2:]:
+    for copy in copies:
         copy.wait()
+    for store in stores:
+        store.start()
     for name, ref in (("in", o_in), ("qkv", o_qkv), ("out", o_out), ("gu", o_gu), ("down", o_down)):
         _, chunk, _, _, which, base = SPECS[name]
         for t, at, width in lane_tiles(chunk):
@@ -588,8 +619,8 @@
     sums, counts = tot_a[5, :NSET], tot_a[5, NSET : 2 * NSET]
     old = running[...]
     o_running[...] = jnp.where(counts > 0.5, 0.75 * old + 0.25 * (sums / jnp.maximum(counts, 1.0)), old)
-    for copy in copies[:2]:
-        copy.wait()
+    for store in stores:
+        store.wait()
 
 
 def hand_out(out, gfeats, tot_a, tot_b, running):
@@ -600,7 +631,8 @@
         out_specs=[HB, HB] + [VM] * 7,
         out_shape=[sd((2, D, LEN), bf16), sd((2, F, LEN), bf16)]
         + [sd((SPECS[n][1],), f32) for n in NAMES] + [sd((2, 9), f32), sd((NSET,), f32)],
-        scratch_shapes=[V((A_ROWS, 128), f32), V((B_ROWS, 128), f32), V((NSET,), f32), pltpu.SemaphoreType.DMA((5,))],
+        scratch_shapes=[V((2, D, LEN), bf16), V((2, F, LEN), bf16), V((A_ROWS, 128), f32), V((B_ROWS, 128), f32), V((NSET,), f32),
+                        pltpu.SemaphoreType.DMA((7,))],
         compiler_params=pltpu.CompilerParams(vmem_limit_bytes=60 * 2**20),
     )(out, gfeats, tot_a, tot_b, running)
 

time: 136 us -> 91.2 us (0.67)
  Pallas kernels: 134 us -> 89.2 us
    pallas_call x1, Pallas kernels: 31.5 us -> 2.81 us  [hand_out(): pl.pallas_call(finish_kernel, in_specs=[HB] * 5, out_specs=[HB, HB] + [VM...]
    pallas_call x1, Pallas kernels: 102 us -> 86.4 us  [run_layer(): pl.pallas_call(layer_kernel, in_specs=[HB] * 4 + [SM] * 2 + [HB] * 9, out...]
where the time goes in v4:
time: 91.2 us; the launch traced here: 90.1 us
  Pallas kernels  89.2 us (98%)
    pallas_call x1, Pallas kernels, run_layer(): pl.pallas_call(layer_kernel, in_specs=[HB] * 4 + [SM] * 2 + [HB] * 9, out...  86.4 us
    pallas_call x1, Pallas kernels, hand_out(): pl.pallas_call(finish_kernel, in_specs=[HB] * 5, out_specs=[HB, HB] + [VM...  2.81 us

profile of v4, /device:TPU:1, one launch (start us, length us, event | category | flops | bytes accessed | tf_op | source)
XLA Modules:
  0.0 90.1 jit_solution(11154870770978488446)
XLA Ops:
  0.6 86.4 %shard_map.223 = (bf16[2,144,1024]{2,1,0:T(8,128)(2,1)}, bf16[2,96,1024]{2,1,0:T(8,128)(2,1)}, f32[8,128]{1,0:T(8,128)}, f32[16,128]{1,0:T(8,128)}) custom-call(bf16[2,96,1024]{2,1,0:T(8,128)(2,1)} %bitcast.5, f32[2,1024]{1,0:T(2,128)} %targets_h.1, s32[2,84]{1,0:T(2,128)} %lag_h.1, s32[2,12]{1,0:T(2,128)} %date_h.1, s32[2]{0:T(128)} %freq.1, s32[2]{0:T(128)} %sets.1, ...), custom_call_target="tpu_custom_call" | custom-call | tf_op jit(solution)/shard_map/pallas_call | solution.py:572
  87.1 2.8 %shard_map.224 = (bf16[2,144,1024]{2,1,0:T(8,128)(2,1)}, bf16[2,96,1024]{2,1,0:T(8,128)(2,1)}, f32[108]{0:T(128)}, f32[486]{0:T(512)}, f32[162]{0:T(256)}, /*ind...) custom-call(bf16[2,144,1024]{2,1,0:T(8,128)(2,1)} %get-tuple-element.22.out_h, ...), custom_call_target="tpu_custom_call" | custom-call | tf_op jit(solution)/shard_map/pallas_call | solution.py:628
